TPU v7x, 128 devices: a whole 4x4x4 slice. The times are simulated.
128 devices in a mesh: view: 4 (over z), tile: 32 (over y, x, core).
Axes of the slice: x: 4, y: 4, z: 4, core: 2. Of those that a mesh axis runs over, the one named last changes fastest.
Arguments:
- features: bfloat16 [8192, 128, 128], P(('view', 'tile')), may hold values from -6 to 6
- block_ids: int32 [4, 32, 128], P('view', 'tile'), may hold values from 0 to 8191, as said below
- weights: bfloat16 [4, 128, 128, 16384], P('view', 'tile'), may hold values from -0.046875 to 0.046875
- decoder: bfloat16 [1152, 512], replicated, may hold values from -0.1875 to 0.1875
- target: bfloat16 [4, 128, 128, 512], P('view', 'tile'), may hold values from -6 to 6
Outputs:
- feature_grad: float32 [8192, 128, 128], P(('view', 'tile'))
- decoder_grad: bfloat16 [1152, 512], replicated
Inputs may be any that keep to these rules, and one draw needn't show every extreme that they name: `block_ids`: A block id b is held by owner b // 64 (owners numbered view-major). In each tile's list at most 2 ids belong to one owner, and some owner has exactly 2. Ids may repeat.
All inputs are finite; a program needn't handle non-finite values.
Results may differ from a plain program's by a relative error of at most 0.0075.
Values may be sent and summed in bfloat16 or wider, within the bound.
A program may use at most 128 MiB of HBM per device.

v0:
```python
import math

import jax
import jax.numpy as jnp
from jax import lax
from jax.sharding import PartitionSpec as P


def with_halo(block, sides, width):
    for axis, dim in sides:
        count = lax.axis_size(axis)
        forward = [(i, i + 1) for i in range(count - 1)]
        backward = [(target, source) for source, target in forward]
        low = lax.ppermute(
            lax.slice_in_dim(block, block.shape[dim] - width, None, axis=dim), axis, forward
        )
        high = lax.ppermute(lax.slice_in_dim(block, 0, width, axis=dim), axis, backward)
        block = jnp.concatenate([low, block, high], axis=dim)
    return block


def body(features, block_ids, weights, decoder, target):
    n_view = lax.axis_size("view")
    n_tile = lax.axis_size("tile")
    owners = n_view * n_tile
    g_dev, block, chans = features.shape
    rows, width, listed = (weights.shape[1], weights.shape[2], weights.shape[3])
    k_len = block_ids.shape[2]
    outs = decoder.shape[1]
    cap = 2 * k_len // owners
    pixels = rows * width
    ids = block_ids[0, 0]
    owner = ids // g_dev
    local = ids - owner * g_dev
    positions = jnp.arange(k_len)
    before = positions[None, :] < positions[:, None]
    rank = jnp.sum(((owner[:, None] == owner[None, :]) & before).astype(jnp.int32), axis=1)
    slot = owner * cap + rank
    place = slot[None, :] == jnp.arange(owners * cap)[:, None]
    request = jnp.sum(jnp.where(place, local[None, :], 0), axis=1).reshape(owners, cap)
    incoming = lax.all_to_all(request, ("view", "tile"), split_axis=0, concat_axis=0, tiled=True)
    outgoing = features[incoming.reshape(-1)].reshape(owners, cap, block, chans)
    arrived = lax.all_to_all(outgoing, ("view", "tile"), split_axis=0, concat_axis=0, tiled=True)
    arrived = arrived.reshape(owners * cap, block, chans)
    gathered = arrived[slot].reshape(listed, chans)
    tile_w = weights.reshape(pixels, listed)
    image = jnp.dot(tile_w, gathered, preferred_element_type=jnp.float32).astype(jnp.bfloat16)
    image = image.reshape(rows, width, chans)
    rimmed = with_halo(image, (("tile", 0),), 1)
    padded = jnp.pad(rimmed, ((0, 0), (1, 1), (0, 0)))
    patches = jnp.concatenate(
        [padded[dy : dy + rows, dx : dx + width, :] for dy in range(3) for dx in range(3)], axis=-1
    )
    patch_rows = patches.reshape(pixels, 9 * chans)
    decoded = jnp.dot(patch_rows, decoder, preferred_element_type=jnp.float32)
    dout = (decoded - target.reshape(pixels, outs).astype(jnp.float32)).astype(jnp.bfloat16)
    scale = 1.0 / math.sqrt(n_view * n_tile * pixels)
    weight_part = lax.dot_general(
        patch_rows, dout, (((0,), (0,)), ((), ())), preferred_element_type=jnp.float32
    )
    decoder_grad = (lax.psum(weight_part, ("view", "tile")) * scale).astype(jnp.bfloat16)
    dout_rim = with_halo(dout.reshape(rows, width, outs), (("tile", 0),), 1)
    dout_pad = jnp.pad(dout_rim, ((0, 0), (1, 1), (0, 0)))
    dpatch = lax.dot_general(
        dout_pad.reshape((rows + 2) * (width + 2), outs),
        decoder,
        (((1,), (1,)), ((), ())),
        preferred_element_type=jnp.float32,
    )
    dpatch = dpatch.reshape(rows + 2, width + 2, 3, 3, chans)
    image_grad = jnp.zeros((rows, width, chans), jnp.float32)
    for dy in range(3):
        for dx in range(3):
            image_grad = (
                image_grad + dpatch[2 - dy : 2 - dy + rows, 2 - dx : 2 - dx + width, dy, dx, :]
            )
    image_grad = image_grad.astype(jnp.bfloat16).reshape(pixels, chans)
    block_grad = lax.dot_general(
        tile_w, image_grad, (((0,), (0,)), ((), ())), preferred_element_type=jnp.float32
    ).astype(jnp.bfloat16)
    returned = (
        jnp.zeros((owners * cap, block, chans), jnp.bfloat16)
        .at[slot]
        .set(block_grad.reshape(k_len, block, chans))
    )
    received = lax.all_to_all(
        returned.reshape(owners, cap, block, chans),
        ("view", "tile"),
        split_axis=0,
        concat_axis=0,
        tiled=True,
    )
    received = received.reshape(owners * cap, block, chans).astype(jnp.float32)
    feature_grad = (
        jnp.zeros((g_dev, block, chans), jnp.float32).at[incoming.reshape(-1)].add(received)
    )
    return (feature_grad, decoder_grad)


def solution(mesh):
    placed = (
        P(("view", "tile"), None, None),
        P("view", "tile", None),
        P("view", "tile", None, None),
        P(),
        P("view", "tile", None, None),
    )
    return jax.shard_map(
        body,
        mesh=mesh,
        in_specs=placed,
        out_specs=(P(("view", "tile"), None, None), P()),
        check_vma=False,
    )
```

profile of v0, /device:TPU:19, one launch (start us, length us, event | category | flops | bytes accessed | tf_op | source)
XLA Modules:
  0.0 542.1 jit_solution(13092389091245386102)
XLA Ops:
  7.2 0.8 bitcast_subtract_fusion
  8.5 17.4 %all_to_all.19 = s32[128,1,2]{2,1,0:T(1,128)S(1)} all-to-all(s32[128,1,2]{2,1,0:T(1,128)S(1)} %bitcast.128), channel_id=1, replica_groups=mesh['view'=4,'tile'=32] {'view','tile'}, dimensions={0} | all-to-all | bytes 2048 | tf_op jit(solution)/shard_map/all_to_all | solution.py:41
  25.8 0.5 broadcast.245
  26.4 0.8 reduce.3
  27.3 8.5 %gather_fusion = bf16[256,128,128]{2,1,0:T(8,128)(2,1)} fusion(bf16[64,128,128]{2,1,0:T(8,128)(2,1)S(1)} %copy-done, s32[1024]{0:T(1024)S(1)} %pad_clamp_fusion.1), kind=kCustom, calls=%fused_computation | custom fusion | bytes 16778240 | tf_op jit(solution)/shard_map/gather | solution.py:42
  35.8 8.3 %all-to-all-start.1 = ((bf16[128,2,128,128]{3,2,1,0:T(8,128)(2,1)}), bf16[128,2,128,128]{3,2,1,0:T(8,128)(2,1)}, u32[]{:S(2)}, u32[]{:S(2)}) async-start(bf16[128,2,128,128]{3,2,1,0:T(8,128)(2,1)} %bitcast.115), calls=%async_computation.1 | async-start | bytes 16777216 | tf_op jit(solution)/shard_map/all_to_all | solution.py:43
  44.2 99.7 %all-to-all-done.1 = bf16[128,2,128,128]{3,2,1,0:T(8,128)(2,1)} async-done(((bf16[128,2,128,128]{3,2,1,0:T(8,128)(2,1)}), bf16[128,2,128,128]{3,2,1,0:T(8,128)(2,1)}, u32[]{:S(2)}, u32[]{:S(2)}) %all-to-all-start.1) | async-done | bytes 8388640 | tf_op jit(solution)/shard_map/all_to_all | solution.py:43
  143.9 6.5 %gather_fusion.1 = bf16[128,128,128]{2,1,0:T(8,128)(2,1)} fusion(bf16[256,128,128]{2,1,0:T(8,128)(2,1)} %bitcast.7, s32[1024]{0:T(1024)S(1)} %pad_clamp_fusion), kind=kCustom, calls=%fused_computation.1 | custom fusion | bytes 8389120 | tf_op jit(solution)/shard_map/gather | solution.py:45
  150.4 12.7 %fusion.3 = bf16[512,128]{0,1:T(8,128)(2,1)S(1)} fusion(bf16[16384,128]{1,0:T(8,128)(2,1)} %bitcast.116, bf16[512,16384]{1,0:T(8,128)(2,1)} %bitcast.112), kind=kOutput, calls=%fused_computation.16 | convolution fusion | flops 2147549184 | bytes 21102592 | tf_op jit(solution)/shard_map/dot_general | solution.py:47
  163.1 4.0 collective-permute-start
  167.1 1.9 collective-permute-start.1
  169.2 3.2 collective-permute-done.1
  172.4 0.7 fusion.24
  173.1 0.3 pad_maximum_fusion
  173.5 0.5 fusion.33
  174.2 0.6 copy-done.2
  174.8 0.9 fusion.2
  175.7 1.9 collective-permute-start.2
  177.7 2.6 collective-permute-start.3
  180.3 3.7 collective-permute-done.3
  184.0 1.3 fusion.11
  185.5 10.2 %fusion = bf16[16384,128]{0,1:T(8,128)(2,1)} fusion(bf16[512,128]{1,0:T(8,128)(2,1)S(1)} %bitcast.119, bf16[512,16384]{1,0:T(8,128)(2,1)} %bitcast.113), kind=kOutput, calls=%fused_computation.5 | convolution fusion | flops 2149580800 | bytes 21102592 | tf_op jit(solution)/shard_map/dot_general | solution.py:78
  195.7 6.3 %copy.29 = bf16[16384,128]{1,0:T(8,128)(2,1)} copy(bf16[16384,128]{0,1:T(8,128)(2,1)} %fusion) | data formatting | bytes 8388608 | tf_op jit(solution)/shard_map/reshape | solution.py:84
  202.0 5.3 broadcast_in_dim.19
  207.4 19.7 %scatter_fusion = bf16[256,128,128]{2,1,0:T(8,128)(2,1)} fusion(bf16[256,128,128]{2,1,0:T(8,128)(2,1)} %broadcast_in_dim.19, s32[128]{0:T(128)S(1)} %fusion.28, bf16[128,128,128]{2,1,0:T(8,128)(2,1)} %bitcast.117), kind=kCustom, calls=%fused_computation.2 | custom fusion | bytes 12583424 | tf_op jit(solution)/shard_map/scatter | solution.py:84
  227.0 13.7 %all-to-all-start.2 = ((bf16[128,2,128,128]{3,2,1,0:T(8,128)(2,1)}), bf16[128,2,128,128]{3,2,1,0:T(8,128)(2,1)}, u32[]{:S(2)}, u32[]{:S(2)}) async-start(bf16[128,2,128,128]{3,2,1,0:T(8,128)(2,1)} %bitcast.114), calls=%async_computation.2 | async-start | bytes 16777216 | tf_op jit(solution)/shard_map/all_to_all | solution.py:86
  240.8 2.2 fusion.34
  243.0 225.0 %all-reduce.4.cloned.1.call-done = f32[1152,512]{1,0:T(8,128)} async-done(((f32[1152,512]{1,0:T(8,128)}), f32[1152,512]{1,0:T(8,128)}) %all-reduce.4.cloned.1.call-update) | async-done | bytes 2359312 | tf_op jit(solution)/shard_map/psum | solution.py:61
  468.0 3.0 multiply_convert_fusion
  471.0 11.2 %bitcast_convert_fusion = f32[256,128,128]{2,1,0:T(8,128)} fusion(bf16[128,2,128,128]{3,2,1,0:T(8,128)(2,1)} %all-to-all-done.2), kind=kLoop, calls=%fused_computation.6 | loop fusion | flops 4194304 | bytes 25165824 | tf_op jit(solution)/shard_map/convert_element_type | solution.py:93
  482.2 2.5 broadcast_in_dim.12
  484.7 50.5 %scatter_fusion.1 = f32[64,128,128]{2,1,0:T(8,128)} fusion(f32[64,128,128]{2,1,0:T(8,128)} %broadcast_in_dim.12, s32[256]{0:T(256)S(1)} %bitcast.130, f32[256,128,128]{2,1,0:T(8,128)} %bitcast_convert_fusion), kind=kCustom, calls=%fused_computation.3 | custom fusion | flops 4194304 | bytes 50332672 | tf_op jit(solution)/shard_map/scatter-add | solution.py:95
  (38 shorter events, 1.3 us)
Async XLA Ops:
  7.2 20.2 %copy-start = (bf16[64,128,128]{2,1,0:T(8,128)(2,1)S(1)}, bf16[64,128,128]{2,1,0:T(8,128)(2,1)}, u32[]{:S(2)}) copy-start(bf16[64,128,128]{2,1,0:T(8,128)(2,1)} %param.5) | copy-start | bytes 6291460
  35.8 8.3 %copy-start.4 = (s32[1,1,128]{2,1,0:T(1,128)S(1)}, s32[1,1,128]{2,1,0:T(1,128)}, u32[]{:S(2)}) copy-start(s32[1,1,128]{2,1,0:T(1,128)} %param.6) | copy-start | bytes 1540
  35.8 108.1 %all-to-all-start.1 = ((bf16[128,2,128,128]{3,2,1,0:T(8,128)(2,1)}), bf16[128,2,128,128]{3,2,1,0:T(8,128)(2,1)}, u32[]{:S(2)}, u32[]{:S(2)}) async-start(bf16[128,2,128,128]{3,2,1,0:T(8,128)(2,1)} %bitcast.115), calls=%async_computation.1 | async-start | bytes 16777216 | tf_op jit(solution)/shard_map/all_to_all | solution.py:43
  163.1 6.0 %collective-permute-start = (bf16[1,128,128]{1,2,0:T(8,128)(2,1)S(1)}, bf16[1,128,128]{1,2,0:T(8,128)(2,1)S(1)}, u32[]{:S(2)}, u32[]{:S(2)}) collective-permute-start(bf16[1,128,128]{1,2,0:T(8,128)(2,1)S(1)} %get-tuple-element.14), channel_id=1, source_target_pairs={{0,1},{1,2},{2,3},{3,4},{4,5},{5,6},{6,7},{7,8},{8,9},{9,10},{10,1... | collective-permute-start | bytes 98312 | tf_op jit(solution)/shard_map/ppermute | solution.py:14
  167.1 5.2 collective-permute-start.1
  173.4 1.3 copy-start.2
  173.5 1.4 copy-start.3
  175.7 4.5 collective-permute-start.2
  177.7 6.3 %collective-permute-start.3 = (bf16[1,128,512]{2,1,0:T(8,128)(2,1)S(1)}, bf16[1,128,512]{2,1,0:T(8,128)(2,1)S(1)}, u32[]{:S(2)}, u32[]{:S(2)}) collective-permute-start(bf16[1,128,512]{2,1,0:T(8,128)(2,1)S(1)} %get-tuple-element.5), channel_id=1, source_target_pairs={{1,0},{2,1},{3,2},{4,3},{5,4},{6,5},{7,6},{8,7},{9,8},{10,9},{11,1... | collective-permute-start | bytes 393224 | tf_op jit(solution)/shard_map/ppermute | solution.py:17
  227.0 244.0 %all-to-all-start.2 = ((bf16[128,2,128,128]{3,2,1,0:T(8,128)(2,1)}), bf16[128,2,128,128]{3,2,1,0:T(8,128)(2,1)}, u32[]{:S(2)}, u32[]{:S(2)}) async-start(bf16[128,2,128,128]{3,2,1,0:T(8,128)(2,1)} %bitcast.114), calls=%async_computation.2 | async-start | bytes 16777216 | tf_op jit(solution)/shard_map/all_to_all | solution.py:86
  240.7 227.3 %all-reduce.4.cloned.1.call-start = ((), (), s32[]{:S(2)}) async-start(), calls=%async_computation.3 | async-start | bytes 4718592 | tf_op jit(solution)/shard_map/psum | solution.py:61
  484.7 50.5 %copy-start.1 = (bf16[64,128,128]{2,1,0:T(8,128)(2,1)S(1)}, bf16[64,128,128]{2,1,0:T(8,128)(2,1)}, u32[]{:S(2)}) copy-start(bf16[64,128,128]{2,1,0:T(8,128)(2,1)} %param.5) | copy-start | bytes 6291460
Sparse Core Ops, SparseCore 0:
  246.9 221.0 all-reduce.3
where the time goes:
time: 547 us; the launch traced here: 542 us
  waiting for transfers between devices  332 us (61%)
  other arithmetic  67.8 us (12%)
  local copies, waits for them, and re-layouts  51.1 us (9%)
  starting transfers between devices  32.5 us (6%)
  matrix products  27.3 us (5%)
  blocking collectives  17.4 us (3%)
  between operations  14.3 us (3%)
    psum x1, waiting for transfers between devices, body(): lax.psum(weight_part, ('view', 'tile')) * scale  225 us
    all_to_all x1, waiting for transfers between devices, body(): lax.all_to_all(outgoing, ('view', 'tile'), split_axis=0, concat_axis=0, t...  99.7 us
    scatter-add x1, other arithmetic, body(): jnp.zeros((g_dev, block, chans), jnp.float32).at[incoming.reshape(-1)]  50.5 us
    scatter x1, local copies, waits for them, and re-layouts, body(): returned = jnp.zeros((owners * cap, block, chans), jnp.bfloat16).at[slot]...  19.7 us
    all_to_all x1, blocking collectives, body(): lax.all_to_all(request, ('view', 'tile'), split_axis=0, concat_axis=0, ti...  17.4 us
    all_to_all x1, starting transfers between devices, body(): lax.all_to_all(returned.reshape(owners, cap, block, chans), ('view', 'til...  13.7 us
    dot_general x1, matrix products, body(): jnp.dot(tile_w, gathered, preferred_element_type=jnp.float32)  12.7 us
    convert_element_type x1, other arithmetic, body(): received = received.reshape(owners * cap, block, chans).astype(jnp.float32)  11.2 us
  transfers between devices with their start and end apart: 7, of which 4 were waited for; matrix products, arithmetic and copies ran while one was open for 1% of the time, Pallas kernels for 0%

commit v1 on v0

--- a/solution.py
+++ b/solution.py
@@ -1,9 +1,14 @@
+import functools
 import math
 
 import jax
 import jax.numpy as jnp
 from jax import lax
+from jax.experimental import pallas as pl
+from jax.experimental.pallas import tpu as pltpu
 from jax.sharding import PartitionSpec as P
+
+GROUP = 8
 
 
 def with_halo(block, sides, width):
@@ -17,6 +22,154 @@
         high = lax.ppermute(lax.slice_in_dim(block, 0, width, axis=dim), axis, backward)
         block = jnp.concatenate([low, block, high], axis=dim)
     return block
+
+
+def pick_kernel(idx_ref, feat_ref, out_ref):
+    step = pl.program_id(0)
+    count = out_ref.shape[0]
+    for j in range(count):
+        out_ref[j] = feat_ref[idx_ref[step * count + j]]
+
+
+def pick(index, features):
+    count = index.shape[0]
+    per = 16
+    tail = features.shape[1:]
+    return pl.pallas_call(
+        pick_kernel,
+        grid_spec=pltpu.PrefetchScalarGridSpec(
+            num_scalar_prefetch=1,
+            grid=(count // per,),
+            in_specs=[pl.BlockSpec(memory_space=pltpu.VMEM)],
+            out_specs=pl.BlockSpec((per, *tail), lambda i, idx: (i, 0, 0)),
+        ),
+        out_shape=jax.ShapeDtypeStruct((count, *tail), features.dtype),
+        compiler_params=pltpu.CompilerParams(vmem_limit_bytes=16 << 20),
+    )(index, features)
+
+
+def composite_kernel(slot_ref, w_ref, *refs):
+    blocks, image_ref, acc = refs[:-2], refs[-2], refs[-1]
+    step = pl.program_id(0)
+
+    @pl.when(step == 0)
+    def _():
+        acc[...] = jnp.zeros_like(acc)
+
+    stacked = jnp.concatenate([b[0] for b in blocks], axis=0)
+    acc[...] += jnp.dot(w_ref[...], stacked, preferred_element_type=jnp.float32)
+
+    @pl.when(step == pl.num_programs(0) - 1)
+    def _():
+        image_ref[...] = acc[...].astype(image_ref.dtype)
+
+
+def composite(slot, tile_w, arrived):
+    pixels, listed = tile_w.shape
+    _, block, chans = arrived.shape
+
+    def at(j):
+        return pl.BlockSpec((1, block, chans), lambda i, s: (s[i * GROUP + j], 0, 0))
+
+    return pl.pallas_call(
+        composite_kernel,
+        grid_spec=pltpu.PrefetchScalarGridSpec(
+            num_scalar_prefetch=1,
+            grid=(listed // (GROUP * block),),
+            in_specs=[pl.BlockSpec((pixels, GROUP * block), lambda i, s: (0, i))]
+            + [at(j) for j in range(GROUP)],
+            out_specs=pl.BlockSpec((pixels, chans), lambda i, s: (0, 0)),
+            scratch_shapes=[pltpu.VMEM((pixels, chans), jnp.float32)],
+        ),
+        out_shape=jax.ShapeDtypeStruct((pixels, chans), jnp.bfloat16),
+        compiler_params=pltpu.CompilerParams(vmem_limit_bytes=16 << 20),
+    )(slot, tile_w, *([arrived] * GROUP))
+
+
+def spread_kernel(slot_ref, w_ref, grad_ref, out_ref, buf, sems):
+    step = pl.program_id(0)
+    last = pl.num_programs(0) - 1
+    half = lax.rem(step, 2)
+    block = buf.shape[2]
+
+    def copy(h, s, j):
+        return pltpu.make_async_copy(
+            buf.at[h, j], out_ref.at[slot_ref[s * GROUP + j]], sems.at[h, j]
+        )
+
+    @pl.when(step >= 2)
+    def _():
+        for j in range(GROUP):
+            copy(half, step - 2, j).wait()
+
+    part = lax.dot_general(
+        grad_ref[...], w_ref[...], (((0,), (0,)), ((), ())), preferred_element_type=jnp.float32
+    )
+    for j in range(GROUP):
+        buf[half, j] = part[:, j * block : (j + 1) * block].T.astype(buf.dtype)
+        copy(half, step, j).start()
+
+    @pl.when(step == last)
+    def _():
+        for j in range(GROUP):
+            copy(1 - half, step - 1, j).wait()
+            copy(half, step, j).wait()
+
+
+def spread(slot, tile_w, image_grad, slots):
+    pixels, listed = tile_w.shape
+    chans = image_grad.shape[1]
+    block = chans
+    return pl.pallas_call(
+        spread_kernel,
+        grid_spec=pltpu.PrefetchScalarGridSpec(
+            num_scalar_prefetch=1,
+            grid=(listed // (GROUP * block),),
+            in_specs=[
+                pl.BlockSpec((pixels, GROUP * block), lambda i, s: (0, i)),
+                pl.BlockSpec((pixels, chans), lambda i, s: (0, 0)),
+            ],
+            out_specs=pl.BlockSpec(memory_space=pl.ANY),
+            scratch_shapes=[
+                pltpu.VMEM((2, GROUP, block, chans), jnp.bfloat16),
+                pltpu.SemaphoreType.DMA((2, GROUP)),
+            ],
+        ),
+        out_shape=jax.ShapeDtypeStruct((slots, block, chans), jnp.bfloat16),
+        compiler_params=pltpu.CompilerParams(vmem_limit_bytes=16 << 20),
+    )(slot, tile_w, image_grad)
+
+
+def add_kernel(idx_ref, in_ref, out_ref):
+    step = pl.program_id(0)
+    count = in_ref.shape[0]
+
+    @pl.when(step == 0)
+    def _():
+        out_ref[...] = jnp.zeros_like(out_ref)
+
+    for j in range(count):
+        where = idx_ref[step * count + j]
+
+        @pl.when(where >= 0)
+        def _():
+            out_ref[where] += in_ref[j].astype(jnp.float32)
+
+
+def add_up(index, received, owned):
+    count, block, chans = received.shape
+    per = 16
+    return pl.pallas_call(
+        add_kernel,
+        grid_spec=pltpu.PrefetchScalarGridSpec(
+            num_scalar_prefetch=1,
+            grid=(count // per,),
+            in_specs=[pl.BlockSpec((per, block, chans), lambda i, idx: (i, 0, 0))],
+            out_specs=pl.BlockSpec((owned, block, chans), lambda i, idx: (0, 0, 0)),
+        ),
+        out_shape=jax.ShapeDtypeStruct((owned, block, chans), jnp.float32),
+        compiler_params=pltpu.CompilerParams(vmem_limit_bytes=24 << 20),
+    )(index, received)
 
 
 def body(features, block_ids, weights, decoder, target):
@@ -37,14 +190,14 @@
     rank = jnp.sum(((owner[:, None] == owner[None, :]) & before).astype(jnp.int32), axis=1)
     slot = owner * cap + rank
     place = slot[None, :] == jnp.arange(owners * cap)[:, None]
-    request = jnp.sum(jnp.where(place, local[None, :], 0), axis=1).reshape(owners, cap)
+    request = jnp.sum(jnp.where(place, local[None, :] + 1, 0), axis=1).reshape(owners, cap) - 1
     incoming = lax.all_to_all(request, ("view", "tile"), split_axis=0, concat_axis=0, tiled=True)
-    outgoing = features[incoming.reshape(-1)].reshape(owners, cap, block, chans)
+    incoming = incoming.reshape(-1)
+    outgoing = pick(jnp.maximum(incoming, 0), features).reshape(owners, cap, block, chans)
     arrived = lax.all_to_all(outgoing, ("view", "tile"), split_axis=0, concat_axis=0, tiled=True)
     arrived = arrived.reshape(owners * cap, block, chans)
-    gathered = arrived[slot].reshape(listed, chans)
     tile_w = weights.reshape(pixels, listed)
-    image = jnp.dot(tile_w, gathered, preferred_element_type=jnp.float32).astype(jnp.bfloat16)
+    image = composite(slot, tile_w, arrived)
     image = image.reshape(rows, width, chans)
     rimmed = with_halo(image, (("tile", 0),), 1)
     padded = jnp.pad(rimmed, ((0, 0), (1, 1), (0, 0)))
@@ -75,14 +228,7 @@
                 image_grad + dpatch[2 - dy : 2 - dy + rows, 2 - dx : 2 - dx + width, dy, dx, :]
             )
     image_grad = image_grad.astype(jnp.bfloat16).reshape(pixels, chans)
-    block_grad = lax.dot_general(
-        tile_w, image_grad, (((0,), (0,)), ((), ())), preferred_element_type=jnp.float32
-    ).astype(jnp.bfloat16)
-    returned = (
-        jnp.zeros((owners * cap, block, chans), jnp.bfloat16)
-        .at[slot]
-        .set(block_grad.reshape(k_len, block, chans))
-    )
+    returned = spread(slot, tile_w, image_grad, owners * cap)
     received = lax.all_to_all(
         returned.reshape(owners, cap, block, chans),
         ("view", "tile"),
@@ -90,10 +236,8 @@
         concat_axis=0,
         tiled=True,
     )
-    received = received.reshape(owners * cap, block, chans).astype(jnp.float32)
-    feature_grad = (
-        jnp.zeros((g_dev, block, chans), jnp.float32).at[incoming.reshape(-1)].add(received)
-    )
+    received = received.reshape(owners * cap, block, chans)
+    feature_grad = add_up(incoming, received, g_dev)
     return (feature_grad, decoder_grad)
 
 

time: 547 us -> 453 us (0.83)
  blocking collectives: 17.4 us -> 119 us
  waiting for transfers between devices: 332 us -> 232 us
  other arithmetic: 67.8 us -> 5.13 us
  Pallas kernels: 0 us -> 46.4 us
  local copies, waits for them, and re-layouts: 51.1 us -> 6.74 us
  matrix products: 27.3 us -> 4.35 us
  starting transfers between devices: 32.5 us -> 22.3 us
    all_to_all x0 -> x1, blocking collectives: none -> 101 us  [body(): lax.all_to_all(outgoing, ('view', 'tile'), split_axis=0, concat_axis=0, t...]
    all_to_all x1 -> x0, waiting for transfers between devices: 99.7 us -> none  [body(): lax.all_to_all(outgoing, ('view', 'tile'), split_axis=0, concat_axis=0, t...]
    scatter-add x1 -> x0, other arithmetic: 50.5 us -> none  [body(): jnp.zeros((g_dev, block, chans), jnp.float32).at[incoming.reshape(-1)]]
    pallas_call x0 -> x4, Pallas kernels: none -> 46.4 us  [the longest x1 23 us: spread(): pl.pallas_call(spread_kernel, grid_spec=pltpu.PrefetchScalarGridSpec(num_...]
    dot_general x2 -> x0, matrix products: 22.9 us -> none  [the longest x1 12.7 us: body(): jnp.dot(tile_w, gathered, preferred_element_type=jnp.float32)]
    scatter x1 -> x0, local copies, waits for them, and re-layouts: 19.7 us -> none  [body(): returned = jnp.zeros((owners * cap, block, chans), jnp.bfloat16).at[slot]...]
    gather x2 -> x0, local copies, waits for them, and re-layouts: 15 us -> none  [the longest x1 8.49 us: body(): outgoing = features[incoming.reshape(-1)].reshape(owners, cap, block, chans)]
    convert_element_type x1 -> x0, other arithmetic: 11.2 us -> none  [body(): received = received.reshape(owners * cap, block, chans).astype(jnp.float32)]
  transfers between devices with their start and end apart: 7 -> 6, of which waited for: 4 -> 3; matrix products, arithmetic and copies ran while one was open for 1% -> 1% of each run, Pallas kernels for 0% -> 0%
where the time goes in v1:
time: 453 us; the launch traced here: 450 us
  waiting for transfers between devices  232 us (51%)
  blocking collectives  119 us (26%)
  Pallas kernels  46.4 us (10%)
  starting transfers between devices  22.3 us (5%)
  between operations  14.3 us (3%)
  local copies, waits for them, and re-layouts  6.74 us (1%)
  other arithmetic  5.13 us (1%)
    psum x1, waiting for transfers between devices, body(): lax.psum(weight_part, ('view', 'tile')) * scale  225 us
    all_to_all x1, blocking collectives, body(): lax.all_to_all(outgoing, ('view', 'tile'), split_axis=0, concat_axis=0, t...  101 us
    pallas_call x1, Pallas kernels, spread(): pl.pallas_call(spread_kernel, grid_spec=pltpu.PrefetchScalarGridSpec(num_...  23 us
    all_to_all x1, blocking collectives, body(): lax.all_to_all(request, ('view', 'tile'), split_axis=0, concat_axis=0, ti...  17.4 us
    pallas_call x1, Pallas kernels, add_up(): pl.pallas_call(add_kernel, grid_spec=pltpu.PrefetchScalarGridSpec(num_sca...  12.8 us
    all_to_all x1, starting transfers between devices, body(): lax.all_to_all(returned.reshape(owners, cap, block, chans), ('view', 'til...  12.1 us
    pallas_call x1, Pallas kernels, composite(): pl.pallas_call(composite_kernel, grid_spec=pltpu.PrefetchScalarGridSpec(n...  9.25 us
  transfers between devices with their start and end apart: 6, of which 3 were waited for; matrix products, arithmetic and copies ran while one was open for 1% of the time, Pallas kernels for 0%

profile of v1, /device:TPU:19, one launch (start us, length us, event | category | flops | bytes accessed | tf_op | source)
XLA Modules:
  0.0 450.2 jit_solution(2794110678890341402)
XLA Ops:
  7.2 0.8 fusion.26
  7.9 0.2 convert_reduce_fusion
  8.1 0.1 select_reduce_fusion
  8.3 0.1 sub.25
  8.4 17.4 %all_to_all.16 = s32[128,1,2]{2,1,0:T(1,128)S(1)} all-to-all(s32[128,1,2]{2,1,0:T(1,128)S(1)} %bitcast.77), channel_id=1, replica_groups=mesh['view'=4,'tile'=32] {'view','tile'}, dimensions={0} | all-to-all | bytes 2048 | tf_op jit(solution)/shard_map/all_to_all | solution.py:194
  25.8 0.5 broadcast.168
  26.3 0.8 reduce.3
  27.1 0.1 reshape.166.idx_ref
  27.3 1.6 copy-done.4
  28.9 1.3 shard_map.68
  30.2 101.4 %all_to_all.17 = bf16[128,2,128,128]{3,2,1,0:T(8,128)(2,1)S(1)} all-to-all(bf16[128,2,128,128]{3,2,1,0:T(8,128)(2,1)S(1)} %bitcast.64), channel_id=1, replica_groups=mesh['view'=4,'tile'=32] {'view','tile'}, dimensions={0} | all-to-all | bytes 16777216 | tf_op jit(solution)/shard_map/all_to_all | solution.py:197
  131.6 9.2 %shard_map.69 = bf16[512,128]{1,0:T(8,128)(2,1)S(1)} custom-call(s32[128]{0:T(128)S(1)} %multiply_add_fusion.slot_ref, bf16[512,16384]{1,0:T(8,128)(2,1)S(1)} %bitcast.61, bf16[256,128,128]{2,1,0:T(8,128)(2,1)S(1)} %bitcast.53, bf16[256,128,128]{2,1,0:T(8,128)(2,1)S(1)} %bitcast.54, bf16[256,128,128]{2,1,0:T(8,128)(2,1)S(1)} %bitcast.55, ...), custom_call_target="tpu_custom_call" | custom-call | tf_op jit(solution)/shard_map/pallas_call | solution.py:74
  140.9 3.9 collective-permute-start
  144.8 1.9 collective-permute-start.1
  146.8 3.3 collective-permute-done.1
  150.1 0.1 fusion.24
  150.1 0.1 fusion.31
  150.7 0.7 copy-done.5
  151.3 0.8 fusion.1
  152.2 1.9 collective-permute-start.2
  154.1 2.4 collective-permute-start.3
  156.6 3.9 collective-permute-done.3
  160.4 1.3 fusion.8
  161.7 0.2 fusion.19
  161.9 23.0 %shard_map.70 = bf16[256,128,128]{2,1,0:T(8,128)(2,1)S(1)} custom-call(s32[128]{0:T(128)S(1)} %multiply_add_fusion.slot_ref, bf16[512,16384]{1,0:T(8,128)(2,1)S(1)} %bitcast.62, bf16[512,128]{1,0:T(8,128)(2,1)S(1)} %bitcast.67), custom_call_target="tpu_custom_call" | custom-call | tf_op jit(solution)/shard_map/pallas_call | solution.py:123
  184.9 3.2 copy-done.3
  188.2 12.1 %all-to-all-start.2 = ((bf16[128,2,128,128]{3,2,1,0:T(8,128)(2,1)}), bf16[128,2,128,128]{3,2,1,0:T(8,128)(2,1)}, u32[]{:S(2)}, u32[]{:S(2)}) async-start(bf16[128,2,128,128]{3,2,1,0:T(8,128)(2,1)} %bitcast.63), calls=%async_computation.2 | async-start | bytes 16777216 | tf_op jit(solution)/shard_map/all_to_all | solution.py:232
  200.3 0.0 all-reduce.4.cloned.1.call-start
  200.3 2.2 fusion.32
  202.6 225.0 %all-reduce.4.cloned.1.call-done = f32[1152,512]{1,0:T(8,128)} async-done(((f32[1152,512]{1,0:T(8,128)}), f32[1152,512]{1,0:T(8,128)}) %all-reduce.4.cloned.1.call-update) | async-done | bytes 2359312 | tf_op jit(solution)/shard_map/psum | solution.py:214
  427.5 3.0 multiply_convert_fusion
  430.5 12.8 %shard_map.71 = f32[64,128,128]{2,1,0:T(8,128)} custom-call(s32[256]{0:T(256)S(1)} %reshape.166.idx_ref, bf16[256,128,128]{2,1,0:T(8,128)(2,1)} %bitcast.26.in_ref), custom_call_target="tpu_custom_call" | custom-call | tf_op jit(solution)/shard_map/pallas_call | solution.py:162
  (28 shorter events, 0.4 us)
Async XLA Ops:
  7.2 143.5 %copy-start = (bf16[1152,512]{1,0:T(8,128)(2,1)S(1)}, bf16[1152,512]{1,0:T(8,128)(2,1)}, u32[]{:S(2)}) copy-start(bf16[1152,512]{1,0:T(8,128)(2,1)} %param.8) | copy-start | bytes 3538948
  27.3 1.6 copy-start.4
  30.2 101.4 %copy-start.2 = (bf16[1,4,128,16384]{3,2,1,0:T(8,128)(2,1)S(1)}, bf16[1,4,128,16384]{3,2,1,0:T(8,128)(2,1)}, u32[]{:S(2)}) copy-start(bf16[1,4,128,16384]{3,2,1,0:T(8,128)(2,1)} %param.7) | copy-start | bytes 50331652
  140.9 5.9 %collective-permute-start = (bf16[1,128,128]{2,1,0:T(8,128)(2,1)S(1)}, bf16[1,128,128]{2,1,0:T(8,128)(2,1)S(1)}, u32[]{:S(2)}, u32[]{:S(2)}) collective-permute-start(bf16[1,128,128]{2,1,0:T(8,128)(2,1)S(1)} %get-tuple-element.14), channel_id=1, source_target_pairs={{0,1},{1,2},{2,3},{3,4},{4,5},{5,6},{6,7},{7,8},{8,9},{9,10},{10,1... | collective-permute-start | bytes 98312 | tf_op jit(solution)/shard_map/ppermute | solution.py:19
  144.8 5.2 %collective-permute-start.1 = (bf16[1,128,128]{2,1,0:T(8,128)(2,1)S(1)}, bf16[1,128,128]{2,1,0:T(8,128)(2,1)S(1)}, u32[]{:S(2)}, u32[]{:S(2)}) collective-permute-start(bf16[1,128,128]{2,1,0:T(8,128)(2,1)S(1)} %get-tuple-element.15), channel_id=1, source_target_pairs={{1,0},{2,1},{3,2},{4,3},{5,4},{6,5},{7,6},{8,7},{9,8},{10,9},{11,1... | collective-permute-start | bytes 98312 | tf_op jit(solution)/shard_map/ppermute | solution.py:22
  150.3 1.0 copy-start.5
  152.2 4.3 collective-permute-start.2
  154.1 6.3 %collective-permute-start.3 = (bf16[1,128,512]{2,1,0:T(8,128)(2,1)S(1)}, bf16[1,128,512]{2,1,0:T(8,128)(2,1)S(1)}, u32[]{:S(2)}, u32[]{:S(2)}) collective-permute-start(bf16[1,128,512]{2,1,0:T(8,128)(2,1)S(1)} %get-tuple-element.5), channel_id=1, source_target_pairs={{1,0},{2,1},{3,2},{4,3},{5,4},{6,5},{7,6},{8,7},{9,8},{10,9},{11,1... | collective-permute-start | bytes 393224 | tf_op jit(solution)/shard_map/ppermute | solution.py:22
  184.9 3.2 copy-start.3
  188.2 242.4 %all-to-all-start.2 = ((bf16[128,2,128,128]{3,2,1,0:T(8,128)(2,1)}), bf16[128,2,128,128]{3,2,1,0:T(8,128)(2,1)}, u32[]{:S(2)}, u32[]{:S(2)}) async-start(bf16[128,2,128,128]{3,2,1,0:T(8,128)(2,1)} %bitcast.63), calls=%async_computation.2 | async-start | bytes 16777216 | tf_op jit(solution)/shard_map/all_to_all | solution.py:232
  200.3 227.3 %all-reduce.4.cloned.1.call-start = ((), (), s32[]{:S(2)}) async-start(), calls=%async_computation.3 | async-start | bytes 4718592 | tf_op jit(solution)/shard_map/psum | solution.py:214
  430.5 12.8 %copy-start.1 = (bf16[1152,512]{1,0:T(8,128)(2,1)S(1)}, bf16[1152,512]{1,0:T(8,128)(2,1)}, u32[]{:S(2)}) copy-start(bf16[1152,512]{1,0:T(8,128)(2,1)} %param.8) | copy-start | bytes 3538948
Sparse Core Ops, SparseCore 0:
  206.5 221.0 all-reduce.3

commit v2 on v1

--- a/solution.py
+++ b/solution.py
@@ -86,58 +86,210 @@
     )(slot, tile_w, *([arrived] * GROUP))
 
 
-def spread_kernel(slot_ref, w_ref, grad_ref, out_ref, buf, sems):
-    step = pl.program_id(0)
-    last = pl.num_programs(0) - 1
-    half = lax.rem(step, 2)
-    block = buf.shape[2]
-
-    def copy(h, s, j):
-        return pltpu.make_async_copy(
-            buf.at[h, j], out_ref.at[slot_ref[s * GROUP + j]], sems.at[h, j]
-        )
-
-    @pl.when(step >= 2)
-    def _():
-        for j in range(GROUP):
-            copy(half, step - 2, j).wait()
-
-    part = lax.dot_general(
-        grad_ref[...], w_ref[...], (((0,), (0,)), ((), ())), preferred_element_type=jnp.float32
-    )
-    for j in range(GROUP):
-        buf[half, j] = part[:, j * block : (j + 1) * block].T.astype(buf.dtype)
-        copy(half, step, j).start()
-
-    @pl.when(step == last)
-    def _():
-        for j in range(GROUP):
-            copy(1 - half, step - 1, j).wait()
-            copy(half, step, j).wait()
-
-
-def spread(slot, tile_w, image_grad, slots):
-    pixels, listed = tile_w.shape
+def at_offset(step, n_view, n_tile):
+    view, tile = lax.axis_index("view"), lax.axis_index("tile")
+    side = n_view
+    rest = step % (n_view * n_tile // 2)
+    first, second, third = rest % side, (rest // side) % side, rest // (side * side)
+    core = (step // (n_view * n_tile // 2) + step) % 2
+    y, x, c = tile // (2 * side), (tile // 2) % side, tile % 2
+    to_y = (y + first + second) % side
+    to_x = (x + first + third + 2 * second) % side
+    return (view + first) % side, (to_y * side + to_x) * 2 + (c + core) % 2
+
+
+def give_back_kernel(
+    scale, listed_ref, w_ref, grad_ref, part_ref, recv_ref, dec_ref,
+    out_buf, pair_buf, mine_buf, piece_buf, send_buf, view_buf,
+    send_sem, recv_sem, dec_send, dec_recv,
+):
+    n_view, n_tile = lax.axis_size("view"), lax.axis_size("tile")
+    owners = n_view * n_tile
+    chips = n_tile // 2
+    view, tile = lax.axis_index("view"), lax.axis_index("tile")
+    me = view * n_tile + tile
+    chip, core = tile // 2, tile % 2
+    block = recv_ref.shape[3]
+    high = piece_buf.shape[1]
+    wide = part_ref.shape[1] // block
+
+    def remote(src, dst, send, recv, v, t):
+        return pltpu.make_async_remote_copy(
+            src_ref=src, dst_ref=dst, send_sem=send, recv_sem=recv,
+            device_id=(v, t), device_id_type=pl.DeviceIdType.MESH,
+        )
+
+    def cols(j):
+        return pl.ds(pl.multiple_of(j * block, block), block)
+
+    def rows(j):
+        return pl.ds(pl.multiple_of(j * high, 16), high)
+
+    def to_pair(i):
+        return remote(
+            part_ref.at[:, cols(2 * i + 1 - core)], pair_buf.at[i],
+            dec_send.at[i], dec_recv.at[i], view, 2 * chip + 1 - core,
+        )
+
+    for i in range(wide // 2):
+        to_pair(i).start()
+
+    flipped = grad_ref[...].astype(jnp.float32).T.astype(jnp.bfloat16)
+
+    def blocks_for(lin):
+        both = jnp.concatenate(
+            [w_ref[:, pl.ds(listed_ref[2 * lin + r] * block, block)] for r in range(2)], axis=1
+        )
+        made = jnp.dot(flipped, both, preferred_element_type=jnp.float32)
+        return [made[:, r * block : (r + 1) * block].T.astype(jnp.bfloat16) for r in range(2)]
+
+    def copy(step):
+        v, t = at_offset(step, n_view, n_tile)
+        lin = v * n_tile + t
+        return lin, remote(
+            out_buf.at[lin], recv_ref.at[me], send_sem.at[step], recv_sem.at[step], v, t
+        )
+
+    def give(step, carry):
+        lin, sending = copy(step)
+        for r, made in enumerate(blocks_for(lin)):
+            out_buf[lin, r] = made
+        sending.start()
+        return carry
+
+    lead = 8
+    lax.fori_loop(1, lead, give, 0)
+    for i in range(wide // 2):
+        to_pair(i).wait()
+
+    def chip_sum(p_chip):
+        p = 2 * p_chip + core
+        r, j = p // wide, p % wide
+        return part_ref[rows(r), cols(j)] + pair_buf[j // 2, rows(r), :]
+
+    base = wide // 2
+
+    def to_plane(step):
+        to = (chip + step) % chips
+        return to, remote(
+            send_buf.at[to], piece_buf.at[chip],
+            dec_send.at[base + step], dec_recv.at[base + step], view, 2 * to + core,
+        )
+
+    def plane_out(step, carry):
+        to, sending = to_plane(step)
+        send_buf[to] = chip_sum(to).astype(jnp.bfloat16)
+        sending.start()
+        return carry
+
+    lax.fori_loop(1, chips, plane_out, 0)
+    piece_buf[chip] = chip_sum(chip).astype(jnp.bfloat16)
+
+    middle = owners // 4
+    lax.fori_loop(lead, middle, give, 0)
+
+    def plane_in(step, carry):
+        to_plane(step)[1].wait()
+        return carry
+
+    lax.fori_loop(1, chips, plane_in, 0)
+    total = piece_buf[0].astype(jnp.float32)
+    for i in range(1, chips):
+        total = total + piece_buf[i].astype(jnp.float32)
+    mine_buf[...] = total
+    view_buf[view] = total
+
+    def to_view(step):
+        return remote(
+            mine_buf, view_buf.at[view],
+            dec_send.at[base + chips + step], dec_recv.at[base + chips + step],
+            (view + step) % n_view, tile,
+        )
+
+    for step in range(1, n_view):
+        to_view(step).start()
+    second = owners // 2
+    lax.fori_loop(middle, second, give, 0)
+    for step in range(1, n_view):
+        to_view(step).wait()
+    whole = view_buf[0]
+    for i in range(1, n_view):
+        whole = whole + view_buf[i]
+    p_rows, p_cols = rows(tile // wide), cols(tile % wide)
+    dec_ref[p_rows, p_cols] = (whole * scale).astype(dec_ref.dtype)
+
+    after = base + chips + n_view
+
+    def spread_out(step):
+        to = (chip + step) % chips
+        return remote(
+            dec_ref.at[p_rows, p_cols], dec_ref.at[p_rows, p_cols],
+            dec_send.at[after + step], dec_recv.at[after + step], view, 2 * to + core,
+        )
+
+    def spread_start(step, carry):
+        spread_out(step).start()
+        return carry
+
+    lax.fori_loop(1, chips, spread_start, 0)
+    lax.fori_loop(second, owners, give, 0)
+    for r, made in enumerate(blocks_for(me)):
+        recv_ref[me, r] = made
+
+    def spread_wait(step, carry):
+        spread_out(step).wait()
+        return carry
+
+    lax.fori_loop(1, chips, spread_wait, 0)
+
+    def to_pair_end(i):
+        part = dec_ref.at[:, cols(2 * i + core)]
+        k = after + chips + i
+        return remote(part, part, dec_send.at[k], dec_recv.at[k], view, 2 * chip + 1 - core)
+
+    for i in range(wide // 2):
+        to_pair_end(i).start()
+
+    def finish(step, carry):
+        copy(step)[1].wait()
+        return carry
+
+    lax.fori_loop(1, owners, finish, 0)
+    for i in range(wide // 2):
+        to_pair_end(i).wait()
+
+
+def give_back(listed, tile_w, image_grad, weight_part, scale):
+    n_view, n_tile = lax.axis_size("view"), lax.axis_size("tile")
+    owners = n_view * n_tile
     chans = image_grad.shape[1]
-    block = chans
+    deep, outs = weight_part.shape
+    wide = outs // chans
+    high = deep * wide // n_tile
+    copies = wide // 2 + n_tile // 2 + n_view + n_tile // 2 + wide // 2
+    vmem = pl.BlockSpec(memory_space=pltpu.VMEM)
     return pl.pallas_call(
-        spread_kernel,
-        grid_spec=pltpu.PrefetchScalarGridSpec(
-            num_scalar_prefetch=1,
-            grid=(listed // (GROUP * block),),
-            in_specs=[
-                pl.BlockSpec((pixels, GROUP * block), lambda i, s: (0, i)),
-                pl.BlockSpec((pixels, chans), lambda i, s: (0, 0)),
-            ],
-            out_specs=pl.BlockSpec(memory_space=pl.ANY),
-            scratch_shapes=[
-                pltpu.VMEM((2, GROUP, block, chans), jnp.bfloat16),
-                pltpu.SemaphoreType.DMA((2, GROUP)),
-            ],
-        ),
-        out_shape=jax.ShapeDtypeStruct((slots, block, chans), jnp.bfloat16),
-        compiler_params=pltpu.CompilerParams(vmem_limit_bytes=16 << 20),
-    )(slot, tile_w, image_grad)
+        functools.partial(give_back_kernel, scale),
+        in_specs=[pl.BlockSpec(memory_space=pltpu.SMEM), vmem, vmem, vmem],
+        out_specs=[vmem, vmem],
+        out_shape=[
+            jax.ShapeDtypeStruct((owners, 2, chans, chans), jnp.bfloat16),
+            jax.ShapeDtypeStruct((deep, outs), jnp.bfloat16),
+        ],
+        scratch_shapes=[
+            pltpu.VMEM((owners, 2, chans, chans), jnp.bfloat16),
+            pltpu.VMEM((wide // 2, deep, chans), jnp.float32),
+            pltpu.VMEM((high, chans), jnp.float32),
+            pltpu.VMEM((n_tile // 2, high, chans), jnp.bfloat16),
+            pltpu.VMEM((n_tile // 2, high, chans), jnp.bfloat16),
+            pltpu.VMEM((n_view, high, chans), jnp.float32),
+            pltpu.SemaphoreType.DMA((owners,)),
+            pltpu.SemaphoreType.DMA((owners,)),
+            pltpu.SemaphoreType.DMA((copies,)),
+            pltpu.SemaphoreType.DMA((copies,)),
+        ],
+        compiler_params=pltpu.CompilerParams(has_side_effects=True, vmem_limit_bytes=56 << 20),
+    )(listed, tile_w, image_grad, weight_part)
 
 
 def add_kernel(idx_ref, in_ref, out_ref):
@@ -211,7 +363,6 @@
     weight_part = lax.dot_general(
         patch_rows, dout, (((0,), (0,)), ((), ())), preferred_element_type=jnp.float32
     )
-    decoder_grad = (lax.psum(weight_part, ("view", "tile")) * scale).astype(jnp.bfloat16)
     dout_rim = with_halo(dout.reshape(rows, width, outs), (("tile", 0),), 1)
     dout_pad = jnp.pad(dout_rim, ((0, 0), (1, 1), (0, 0)))
     dpatch = lax.dot_general(
@@ -228,14 +379,8 @@
                 image_grad + dpatch[2 - dy : 2 - dy + rows, 2 - dx : 2 - dx + width, dy, dx, :]
             )
     image_grad = image_grad.astype(jnp.bfloat16).reshape(pixels, chans)
-    returned = spread(slot, tile_w, image_grad, owners * cap)
-    received = lax.all_to_all(
-        returned.reshape(owners, cap, block, chans),
-        ("view", "tile"),
-        split_axis=0,
-        concat_axis=0,
-        tiled=True,
-    )
+    in_slot = jnp.sum(jnp.where(place, positions[None, :], 0), axis=1)
+    received, decoder_grad = give_back(in_slot, tile_w, image_grad, weight_part, scale)
     received = received.reshape(owners * cap, block, chans)
     feature_grad = add_up(incoming, received, g_dev)
     return (feature_grad, decoder_grad)

time: 453 us -> 311 us (0.69)
  waiting for transfers between devices: 232 us -> 4.96 us
  Pallas kernels: 46.4 us -> 155 us
  between operations: 14.3 us -> 0.9 us
  starting transfers between devices: 22.3 us -> 10.2 us
    psum x1 -> x0, waiting for transfers between devices: 225 us -> none  [body(): lax.psum(weight_part, ('view', 'tile')) * scale]
    pallas_call x1, Pallas kernels: 23 us -> 139 us  [give_back(): pl.pallas_call(functools.partial(give_back_kernel, scale), in_specs=[pl.B...]
    all_to_all x1 -> x0, starting transfers between devices: 12.1 us -> none  [body(): lax.all_to_all(returned.reshape(owners, cap, block, chans), ('view', 'til...]
    pallas_call x1, Pallas kernels: 12.8 us -> 5.78 us  [add_up(): pl.pallas_call(add_kernel, grid_spec=pltpu.PrefetchScalarGridSpec(num_sca...]
  transfers between devices with their start and end apart: 6 -> 4, of which waited for: 3 -> 2; matrix products, arithmetic and copies ran while one was open for 1% -> 1% of each run, Pallas kernels for 0% -> 0%
where the time goes in v2:
time: 311 us; the launch traced here: 306 us
  Pallas kernels  155 us (50%)
  blocking collectives  119 us (38%)
  starting transfers between devices  10.2 us (3%)
  local copies, waits for them, and re-layouts  7.9 us (3%)
  waiting for transfers between devices  4.96 us (2%)
  matrix products  4.35 us (1%)
  other arithmetic  3.36 us (1%)
    pallas_call x1, Pallas kernels, give_back(): pl.pallas_call(functools.partial(give_back_kernel, scale), in_specs=[pl.B...  139 us
    all_to_all x1, blocking collectives, body(): lax.all_to_all(outgoing, ('view', 'tile'), split_axis=0, concat_axis=0, t...  101 us
    all_to_all x1, blocking collectives, body(): lax.all_to_all(request, ('view', 'tile'), split_axis=0, concat_axis=0, ti...  17.4 us
    pallas_call x1, Pallas kernels, composite(): pl.pallas_call(composite_kernel, grid_spec=pltpu.PrefetchScalarGridSpec(n...  9.24 us
    unnamed x21, local copies, waits for them, and re-layouts  6.92 us
  transfers between devices with their start and end apart: 4, of which 2 were waited for; matrix products, arithmetic and copies ran while one was open for 1% of the time, Pallas kernels for 0%

profile of v2, /device:TPU:19, one launch (start us, length us, event | category | flops | bytes accessed | tf_op | source)
XLA Modules:
  0.0 305.9 jit_solution(8624287252969363618)
XLA Ops:
  0.6 0.0 copy-start
  0.6 0.8 fusion.26
  1.4 0.2 convert_reduce_fusion
  1.6 0.7 select_reduce_fusion
  2.3 0.1 sub.25
  2.4 17.4 %all_to_all.11 = s32[128,1,2]{2,1,0:T(1,128)S(1)} all-to-all(s32[128,1,2]{2,1,0:T(1,128)S(1)} %bitcast.76), channel_id=1, replica_groups=mesh['view'=4,'tile'=32] {'view','tile'}, dimensions={0} | all-to-all | bytes 2048 | tf_op jit(solution)/shard_map/all_to_all | solution.py:346
  19.8 0.5 broadcast.168
  20.3 0.8 reduce.3
  21.1 0.1 reshape.163.idx_ref
  21.3 0.0 copy-start.3
  21.3 1.6 copy-done.3
  22.9 1.3 shard_map.68
  24.2 0.0 copy-start.1
  24.2 101.4 %all_to_all.12 = bf16[128,2,128,128]{3,2,1,0:T(8,128)(2,1)S(1)} all-to-all(bf16[128,2,128,128]{3,2,1,0:T(8,128)(2,1)S(1)} %bitcast.62), channel_id=1, replica_groups=mesh['view'=4,'tile'=32] {'view','tile'}, dimensions={0} | all-to-all | bytes 16777216 | tf_op jit(solution)/shard_map/all_to_all | solution.py:349
  125.6 9.2 %shard_map.69 = bf16[512,128]{1,0:T(8,128)(2,1)S(1)} custom-call(s32[128]{0:T(128)S(1)} %multiply_add_fusion.slot_ref, bf16[512,16384]{1,0:T(8,128)(2,1)S(1)} %bitcast.61, bf16[256,128,128]{2,1,0:T(8,128)(2,1)S(1)} %bitcast.52, bf16[256,128,128]{2,1,0:T(8,128)(2,1)S(1)} %bitcast.53, bf16[256,128,128]{2,1,0:T(8,128)(2,1)S(1)} %bitcast.54, ...), custom_call_target="tpu_custom_call" | custom-call | tf_op jit(solution)/shard_map/pallas_call | solution.py:74
  134.9 3.9 %collective-permute-start = (bf16[1,128,128]{2,1,0:T(8,128)(2,1)S(1)}, bf16[1,128,128]{2,1,0:T(8,128)(2,1)S(1)}, u32[]{:S(2)}, u32[]{:S(2)}) collective-permute-start(bf16[1,128,128]{2,1,0:T(8,128)(2,1)S(1)} %get-tuple-element.20), channel_id=1, source_target_pairs={{0,1},{1,2},{2,3},{3,4},{4,5},{5,6},{6,7},{7,8},{8,9},{9,10},{10,1... | collective-permute-start | bytes 98312 | tf_op jit(solution)/shard_map/ppermute | solution.py:19
  138.8 1.9 collective-permute-start.1
  140.8 3.3 %collective-permute-done.1 = bf16[1,128,128]{2,1,0:T(8,128)(2,1)S(1)} collective-permute-done((bf16[1,128,128]{2,1,0:T(8,128)(2,1)S(1)}, bf16[1,128,128]{2,1,0:T(8,128)(2,1)S(1)}, u32[]{:S(2)}, u32[]{:S(2)}) %collective-permute-start.1) | collective-permute-done | bytes 32800 | tf_op jit(solution)/shard_map/ppermute | solution.py:22
  144.1 0.1 fusion.24
  144.1 0.1 fusion.31
  144.7 0.7 copy-done.5
  145.4 0.8 fusion.1
  146.2 1.9 collective-permute-start.2
  148.2 2.4 collective-permute-start.3
  150.6 2.2 fusion.32.part_ref
  152.8 1.7 collective-permute-done.3
  154.5 1.3 fusion.8
  155.8 0.8 fusion.19
  156.6 139.1 %shard_map.70 = (bf16[128,2,128,128]{3,2,1,0:T(8,128)(2,1)}, bf16[1152,512]{1,0:T(8,128)(2,1)}) custom-call(s32[256]{0:T(256)} %get-tuple-element.6.listed_ref, bf16[512,16384]{1,0:T(8,128)(2,1)} %bitcast.60, bf16[512,128]{1,0:T(8,128)(2,1)} %bitcast.67, f32[1152,512]{1,0:T(8,128)} %fusion.32.part_ref), custom_call_target="tpu_custom_call" | custom-call | tf_op jit(solution)/shard_map/pallas_call | solution.py:271
  295.7 3.4 %copy-done.2 = bf16[128,2,128,128]{3,2,1,0:T(8,128)(2,1)S(1)} copy-done((bf16[128,2,128,128]{3,2,1,0:T(8,128)(2,1)S(1)}, bf16[128,2,128,128]{3,2,1,0:T(8,128)(2,1)}, u32[]{:S(2)}) %copy-start.2) | copy-done | bytes 8388632
  299.1 5.8 %shard_map.71 = f32[64,128,128]{2,1,0:T(8,128)} custom-call(s32[256]{0:T(256)S(1)} %reshape.163.idx_ref, bf16[256,128,128]{2,1,0:T(8,128)(2,1)S(1)} %bitcast.63), custom_call_target="tpu_custom_call" | custom-call | tf_op jit(solution)/shard_map/pallas_call | solution.py:314
  304.8 1.0 copy.19
  (23 shorter events, 0.4 us)
Async XLA Ops:
  0.6 144.1 %copy-start = (bf16[1152,512]{1,0:T(8,128)(2,1)S(1)}, bf16[1152,512]{1,0:T(8,128)(2,1)}, u32[]{:S(2)}) copy-start(bf16[1152,512]{1,0:T(8,128)(2,1)} %param.8) | copy-start | bytes 3538948
  21.3 1.6 copy-start.3
  24.2 101.4 %copy-start.1 = (bf16[1,4,128,16384]{3,2,1,0:T(8,128)(2,1)S(1)}, bf16[1,4,128,16384]{3,2,1,0:T(8,128)(2,1)}, u32[]{:S(2)}) copy-start(bf16[1,4,128,16384]{3,2,1,0:T(8,128)(2,1)} %param.7) | copy-start | bytes 50331652
  134.9 5.9 %collective-permute-start = (bf16[1,128,128]{2,1,0:T(8,128)(2,1)S(1)}, bf16[1,128,128]{2,1,0:T(8,128)(2,1)S(1)}, u32[]{:S(2)}, u32[]{:S(2)}) collective-permute-start(bf16[1,128,128]{2,1,0:T(8,128)(2,1)S(1)} %get-tuple-element.20), channel_id=1, source_target_pairs={{0,1},{1,2},{2,3},{3,4},{4,5},{5,6},{6,7},{7,8},{8,9},{9,10},{10,1... | collective-permute-start | bytes 98312 | tf_op jit(solution)/shard_map/ppermute | solution.py:19
  138.8 5.2 %collective-permute-start.1 = (bf16[1,128,128]{2,1,0:T(8,128)(2,1)S(1)}, bf16[1,128,128]{2,1,0:T(8,128)(2,1)S(1)}, u32[]{:S(2)}, u32[]{:S(2)}) collective-permute-start(bf16[1,128,128]{2,1,0:T(8,128)(2,1)S(1)} %get-tuple-element.21), channel_id=1, source_target_pairs={{1,0},{2,1},{3,2},{4,3},{5,4},{6,5},{7,6},{8,7},{9,8},{10,9},{11,1... | collective-permute-start | bytes 98312 | tf_op jit(solution)/shard_map/ppermute | solution.py:22
  144.3 1.0 copy-start.5
  146.2 6.6 %collective-permute-start.2 = (bf16[1,128,512]{2,1,0:T(8,128)(2,1)S(1)}, bf16[1,128,512]{2,1,0:T(8,128)(2,1)S(1)}, u32[]{:S(2)}, u32[]{:S(2)}) collective-permute-start(bf16[1,128,512]{2,1,0:T(8,128)(2,1)S(1)} %get-tuple-element.10), channel_id=1, source_target_pairs={{0,1},{1,2},{2,3},{3,4},{4,5},{5,6},{6,7},{7,8},{8,9},{9,10},{10,1... | collective-permute-start | bytes 393224 | tf_op jit(solution)/shard_map/ppermute | solution.py:19
  148.2 6.3 %collective-permute-start.3 = (bf16[1,128,512]{2,1,0:T(8,128)(2,1)S(1)}, bf16[1,128,512]{2,1,0:T(8,128)(2,1)S(1)}, u32[]{:S(2)}, u32[]{:S(2)}) collective-permute-start(bf16[1,128,512]{2,1,0:T(8,128)(2,1)S(1)} %get-tuple-element.11), channel_id=1, source_target_pairs={{1,0},{2,1},{3,2},{4,3},{5,4},{6,5},{7,6},{8,7},{9,8},{10,9},{11,1... | collective-permute-start | bytes 393224 | tf_op jit(solution)/shard_map/ppermute | solution.py:22
  295.7 3.4 %copy-start.2 = (bf16[128,2,128,128]{3,2,1,0:T(8,128)(2,1)S(1)}, bf16[128,2,128,128]{3,2,1,0:T(8,128)(2,1)}, u32[]{:S(2)}) copy-start(bf16[128,2,128,128]{3,2,1,0:T(8,128)(2,1)} %get-tuple-element.4) | copy-start | bytes 25165828
  299.1 5.8 %copy-start.4 = (bf16[1152,512]{1,0:T(8,128)(2,1)S(1)}, bf16[1152,512]{1,0:T(8,128)(2,1)}, u32[]{:S(2)}) copy-start(bf16[1152,512]{1,0:T(8,128)(2,1)} %get-tuple-element.25) | copy-start | bytes 3538948

commit v3 on v2

--- a/solution.py
+++ b/solution.py
@@ -9,19 +9,6 @@
 from jax.sharding import PartitionSpec as P
 
 GROUP = 8
-
-
-def with_halo(block, sides, width):
-    for axis, dim in sides:
-        count = lax.axis_size(axis)
-        forward = [(i, i + 1) for i in range(count - 1)]
-        backward = [(target, source) for source, target in forward]
-        low = lax.ppermute(
-            lax.slice_in_dim(block, block.shape[dim] - width, None, axis=dim), axis, forward
-        )
-        high = lax.ppermute(lax.slice_in_dim(block, 0, width, axis=dim), axis, backward)
-        block = jnp.concatenate([low, block, high], axis=dim)
-    return block
 
 
 def pick_kernel(idx_ref, feat_ref, out_ref):
@@ -48,44 +35,6 @@
     )(index, features)
 
 
-def composite_kernel(slot_ref, w_ref, *refs):
-    blocks, image_ref, acc = refs[:-2], refs[-2], refs[-1]
-    step = pl.program_id(0)
-
-    @pl.when(step == 0)
-    def _():
-        acc[...] = jnp.zeros_like(acc)
-
-    stacked = jnp.concatenate([b[0] for b in blocks], axis=0)
-    acc[...] += jnp.dot(w_ref[...], stacked, preferred_element_type=jnp.float32)
-
-    @pl.when(step == pl.num_programs(0) - 1)
-    def _():
-        image_ref[...] = acc[...].astype(image_ref.dtype)
-
-
-def composite(slot, tile_w, arrived):
-    pixels, listed = tile_w.shape
-    _, block, chans = arrived.shape
-
-    def at(j):
-        return pl.BlockSpec((1, block, chans), lambda i, s: (s[i * GROUP + j], 0, 0))
-
-    return pl.pallas_call(
-        composite_kernel,
-        grid_spec=pltpu.PrefetchScalarGridSpec(
-            num_scalar_prefetch=1,
-            grid=(listed // (GROUP * block),),
-            in_specs=[pl.BlockSpec((pixels, GROUP * block), lambda i, s: (0, i))]
-            + [at(j) for j in range(GROUP)],
-            out_specs=pl.BlockSpec((pixels, chans), lambda i, s: (0, 0)),
-            scratch_shapes=[pltpu.VMEM((pixels, chans), jnp.float32)],
-        ),
-        out_shape=jax.ShapeDtypeStruct((pixels, chans), jnp.bfloat16),
-        compiler_params=pltpu.CompilerParams(vmem_limit_bytes=16 << 20),
-    )(slot, tile_w, *([arrived] * GROUP))
-
-
 def at_offset(step, n_view, n_tile):
     view, tile = lax.axis_index("view"), lax.axis_index("tile")
     side = n_view
@@ -98,10 +47,11 @@
     return (view + first) % side, (to_y * side + to_x) * 2 + (c + core) % 2
 
 
-def give_back_kernel(
-    scale, listed_ref, w_ref, grad_ref, part_ref, recv_ref, dec_ref,
+def train_kernel(
+    scale, slot_ref, listed_ref, w_ref, arrived_ref, dec_w_ref, target_ref, recv_ref, dec_ref,
+    acc, rows_buf, target_buf, part_ref,
     out_buf, pair_buf, mine_buf, piece_buf, send_buf, view_buf,
-    send_sem, recv_sem, dec_send, dec_recv,
+    send_sem, recv_sem, dec_send, dec_recv, halo_send, halo_recv, own_sem,
 ):
     n_view, n_tile = lax.axis_size("view"), lax.axis_size("tile")
     owners = n_view * n_tile
@@ -112,6 +62,8 @@
     block = recv_ref.shape[3]
     high = piece_buf.shape[1]
     wide = part_ref.shape[1] // block
+    pixels = w_ref.shape[0]
+    width = block
 
     def remote(src, dst, send, recv, v, t):
         return pltpu.make_async_remote_copy(
@@ -125,6 +77,77 @@
     def rows(j):
         return pl.ds(pl.multiple_of(j * high, 16), high)
 
+    right, left = (tile + 1) % n_tile, (tile + n_tile - 1) % n_tile
+    two = 2 * width
+
+    def halo(buf, i, src, size, dst, to):
+        return remote(
+            buf.at[pl.ds(src, size)], buf.at[pl.ds(dst, size)],
+            halo_send.at[i], halo_recv.at[i], view, to,
+        )
+
+    target_buf[width : width + pixels, :] = target_ref[...]
+    target_halos = [
+        halo(target_buf, 0, pixels, width, 0, right),
+        halo(target_buf, 1, width, width, width + pixels, left),
+    ]
+    for one in target_halos:
+        one.start()
+
+    acc[...] = jnp.zeros_like(acc)
+
+    def add_group(i, carry):
+        stacked = jnp.concatenate(
+            [arrived_ref[slot_ref[i * GROUP + j]] for j in range(GROUP)], axis=0
+        )
+        columns = pl.ds(pl.multiple_of(i * (GROUP * block), GROUP * block), GROUP * block)
+        acc[...] += jnp.dot(w_ref[:, columns], stacked, preferred_element_type=jnp.float32)
+        return carry
+
+    lax.fori_loop(0, w_ref.shape[1] // (GROUP * block), add_group, 0)
+    rows_buf[two : two + pixels, :] = acc[...].astype(jnp.bfloat16)
+    image_halos = [
+        halo(rows_buf, 2, pixels, two, 0, right),
+        halo(rows_buf, 3, two, two, two + pixels, left),
+    ]
+    for one in image_halos:
+        one.start()
+    for one in target_halos + image_halos:
+        one.wait()
+
+    padded = pixels + 4 * width
+    first, last = tile == 0, tile == n_tile - 1
+    place = lax.broadcasted_iota(jnp.int32, (padded, block), 0)
+    outside = (first & (place < two)) | (last & (place >= two + pixels))
+    image = jnp.where(outside, 0.0, rows_buf[...].astype(jnp.float32))
+    column = place % width
+    before = jnp.where(column == 0, 0.0, pltpu.roll(image, 1, 0))
+    after_px = jnp.where(column == width - 1, 0.0, pltpu.roll(image, padded - 1, 0))
+    shifted = jnp.concatenate(
+        [a.astype(jnp.bfloat16) for a in (before, image, after_px)], axis=1
+    )
+    trans = jnp.concatenate(
+        [a.T.astype(jnp.bfloat16) for a in (before, image, after_px)], axis=0
+    )
+    outs = dec_w_ref.shape[1]
+    deep = 3 * block
+    inner = pixels + two
+    decoded = -target_buf[...].astype(jnp.float32)
+    for dy in range(3):
+        decoded = decoded + jnp.dot(
+            shifted[dy * width : dy * width + inner], dec_w_ref[dy * deep : (dy + 1) * deep, :],
+            preferred_element_type=jnp.float32,
+        )
+    place = lax.broadcasted_iota(jnp.int32, (inner, outs), 0)
+    outside = (first & (place < width)) | (last & (place >= width + pixels))
+    dout = jnp.where(outside, 0.0, decoded).astype(jnp.bfloat16)
+    own = dout[width : width + pixels]
+    for dy in range(3):
+        low = (1 + dy) * width
+        part_ref[dy * deep : (dy + 1) * deep, :] = jnp.dot(
+            trans[:, low : low + pixels], own, preferred_element_type=jnp.float32
+        )
+
     def to_pair(i):
         return remote(
             part_ref.at[:, cols(2 * i + 1 - core)], pair_buf.at[i],
@@ -134,7 +157,18 @@
     for i in range(wide // 2):
         to_pair(i).start()
 
-    flipped = grad_ref[...].astype(jnp.float32).T.astype(jnp.bfloat16)
+    spread = jnp.zeros((pixels, deep), jnp.float32)
+    for dy in range(3):
+        low = (2 - dy) * width
+        spread = spread + lax.dot_general(
+            dout[low : low + pixels], dec_w_ref[dy * deep : (dy + 1) * deep, :],
+            (((1,), (1,)), ((), ())), preferred_element_type=jnp.float32,
+        )
+    column = lax.broadcasted_iota(jnp.int32, (pixels, block), 0) % width
+    later = jnp.where(column == width - 1, 0.0, pltpu.roll(spread[:, :block], pixels - 1, 0))
+    earlier = jnp.where(column == 0, 0.0, pltpu.roll(spread[:, 2 * block :], 1, 0))
+    image_grad = (later + spread[:, block : 2 * block] + earlier).astype(jnp.bfloat16)
+    flipped = image_grad.astype(jnp.float32).T.astype(jnp.bfloat16)
 
     def blocks_for(lin):
         both = jnp.concatenate(
@@ -234,7 +268,9 @@
     lax.fori_loop(1, chips, spread_start, 0)
     lax.fori_loop(second, owners, give, 0)
     for r, made in enumerate(blocks_for(me)):
-        recv_ref[me, r] = made
+        out_buf[me, r] = made
+    own_copy = pltpu.make_async_copy(out_buf.at[me], recv_ref.at[me], own_sem)
+    own_copy.start()
 
     def spread_wait(step, carry):
         spread_out(step).wait()
@@ -255,28 +291,35 @@
         return carry
 
     lax.fori_loop(1, owners, finish, 0)
+    own_copy.wait()
     for i in range(wide // 2):
         to_pair_end(i).wait()
 
 
-def give_back(listed, tile_w, image_grad, weight_part, scale):
+def train(slot, listed, tile_w, arrived, decoder, target, scale):
     n_view, n_tile = lax.axis_size("view"), lax.axis_size("tile")
     owners = n_view * n_tile
-    chans = image_grad.shape[1]
-    deep, outs = weight_part.shape
+    pixels = tile_w.shape[0]
+    chans = arrived.shape[2]
+    deep, outs = decoder.shape
     wide = outs // chans
     high = deep * wide // n_tile
     copies = wide // 2 + n_tile // 2 + n_view + n_tile // 2 + wide // 2
     vmem = pl.BlockSpec(memory_space=pltpu.VMEM)
+    smem = pl.BlockSpec(memory_space=pltpu.SMEM)
     return pl.pallas_call(
-        functools.partial(give_back_kernel, scale),
-        in_specs=[pl.BlockSpec(memory_space=pltpu.SMEM), vmem, vmem, vmem],
-        out_specs=[vmem, vmem],
+        functools.partial(train_kernel, scale),
+        in_specs=[smem, smem, vmem, vmem, vmem, vmem],
+        out_specs=[pl.BlockSpec(memory_space=pl.ANY), vmem],
         out_shape=[
             jax.ShapeDtypeStruct((owners, 2, chans, chans), jnp.bfloat16),
             jax.ShapeDtypeStruct((deep, outs), jnp.bfloat16),
         ],
         scratch_shapes=[
+            pltpu.VMEM((pixels, chans), jnp.float32),
+            pltpu.VMEM((pixels + 4 * chans, chans), jnp.bfloat16),
+            pltpu.VMEM((pixels + 2 * chans, outs), jnp.bfloat16),
+            pltpu.VMEM((deep, outs), jnp.float32),
             pltpu.VMEM((owners, 2, chans, chans), jnp.bfloat16),
             pltpu.VMEM((wide // 2, deep, chans), jnp.float32),
             pltpu.VMEM((high, chans), jnp.float32),
@@ -287,25 +330,32 @@
             pltpu.SemaphoreType.DMA((owners,)),
             pltpu.SemaphoreType.DMA((copies,)),
             pltpu.SemaphoreType.DMA((copies,)),
+            pltpu.SemaphoreType.DMA((4,)),
+            pltpu.SemaphoreType.DMA((4,)),
+            pltpu.SemaphoreType.DMA,
         ],
-        compiler_params=pltpu.CompilerParams(has_side_effects=True, vmem_limit_bytes=56 << 20),
-    )(listed, tile_w, image_grad, weight_part)
-
-
-def add_kernel(idx_ref, in_ref, out_ref):
+        compiler_params=pltpu.CompilerParams(has_side_effects=True, vmem_limit_bytes=58 << 20),
+    )(slot, listed, tile_w, arrived, decoder, target)
+
+
+def add_kernel(idx_ref, in_ref, out_ref, acc, sem):
     step = pl.program_id(0)
     count = in_ref.shape[0]
+    owned = out_ref.shape[0]
 
     @pl.when(step == 0)
     def _():
-        out_ref[...] = jnp.zeros_like(out_ref)
+        acc[...] = jnp.zeros_like(acc)
 
     for j in range(count):
         where = idx_ref[step * count + j]
-
-        @pl.when(where >= 0)
-        def _():
-            out_ref[where] += in_ref[j].astype(jnp.float32)
+        acc[where] += in_ref[j].astype(jnp.float32)
+
+    @pl.when(step == pl.num_programs(0) - 1)
+    def _():
+        copy = pltpu.make_async_copy(acc.at[pl.ds(0, owned)], out_ref, sem)
+        copy.start()
+        copy.wait()
 
 
 def add_up(index, received, owned):
@@ -317,10 +367,14 @@
             num_scalar_prefetch=1,
             grid=(count // per,),
             in_specs=[pl.BlockSpec((per, block, chans), lambda i, idx: (i, 0, 0))],
-            out_specs=pl.BlockSpec((owned, block, chans), lambda i, idx: (0, 0, 0)),
+            out_specs=pl.BlockSpec(memory_space=pl.ANY),
+            scratch_shapes=[
+                pltpu.VMEM((owned + 1, block, chans), jnp.float32),
+                pltpu.SemaphoreType.DMA,
+            ],
         ),
         out_shape=jax.ShapeDtypeStruct((owned, block, chans), jnp.float32),
-        compiler_params=pltpu.CompilerParams(vmem_limit_bytes=24 << 20),
+        compiler_params=pltpu.CompilerParams(vmem_limit_bytes=58 << 20),
     )(index, received)
 
 
@@ -331,7 +385,6 @@
     g_dev, block, chans = features.shape
     rows, width, listed = (weights.shape[1], weights.shape[2], weights.shape[3])
     k_len = block_ids.shape[2]
-    outs = decoder.shape[1]
     cap = 2 * k_len // owners
     pixels = rows * width
     ids = block_ids[0, 0]
@@ -349,40 +402,13 @@
     arrived = lax.all_to_all(outgoing, ("view", "tile"), split_axis=0, concat_axis=0, tiled=True)
     arrived = arrived.reshape(owners * cap, block, chans)
     tile_w = weights.reshape(pixels, listed)
-    image = composite(slot, tile_w, arrived)
-    image = image.reshape(rows, width, chans)
-    rimmed = with_halo(image, (("tile", 0),), 1)
-    padded = jnp.pad(rimmed, ((0, 0), (1, 1), (0, 0)))
-    patches = jnp.concatenate(
-        [padded[dy : dy + rows, dx : dx + width, :] for dy in range(3) for dx in range(3)], axis=-1
+    scale = 1.0 / math.sqrt(n_view * n_tile * pixels)
+    in_slot = jnp.sum(jnp.where(place, positions[None, :], 0), axis=1)
+    received, decoder_grad = train(
+        slot, in_slot, tile_w, arrived, decoder, target.reshape(pixels, -1), scale
     )
-    patch_rows = patches.reshape(pixels, 9 * chans)
-    decoded = jnp.dot(patch_rows, decoder, preferred_element_type=jnp.float32)
-    dout = (decoded - target.reshape(pixels, outs).astype(jnp.float32)).astype(jnp.bfloat16)
-    scale = 1.0 / math.sqrt(n_view * n_tile * pixels)
-    weight_part = lax.dot_general(
-        patch_rows, dout, (((0,), (0,)), ((), ())), preferred_element_type=jnp.float32
-    )
-    dout_rim = with_halo(dout.reshape(rows, width, outs), (("tile", 0),), 1)
-    dout_pad = jnp.pad(dout_rim, ((0, 0), (1, 1), (0, 0)))
-    dpatch = lax.dot_general(
-        dout_pad.reshape((rows + 2) * (width + 2), outs),
-        decoder,
-        (((1,), (1,)), ((), ())),
-        preferred_element_type=jnp.float32,
-    )
-    dpatch = dpatch.reshape(rows + 2, width + 2, 3, 3, chans)
-    image_grad = jnp.zeros((rows, width, chans), jnp.float32)
-    for dy in range(3):
-        for dx in range(3):
-            image_grad = (
-                image_grad + dpatch[2 - dy : 2 - dy + rows, 2 - dx : 2 - dx + width, dy, dx, :]
-            )
-    image_grad = image_grad.astype(jnp.bfloat16).reshape(pixels, chans)
-    in_slot = jnp.sum(jnp.where(place, positions[None, :], 0), axis=1)
-    received, decoder_grad = give_back(in_slot, tile_w, image_grad, weight_part, scale)
     received = received.reshape(owners * cap, block, chans)
-    feature_grad = add_up(incoming, received, g_dev)
+    feature_grad = add_up(jnp.where(incoming < 0, g_dev, incoming), received, g_dev)
     return (feature_grad, decoder_grad)
 
 

time: 311 us -> 300 us (0.965); the launches traced: 306 us -> 300 us
  Pallas kernels: 155 us -> 174 us
  starting transfers between devices: 10.2 us -> 0 us
  waiting for transfers between devices: 4.96 us -> 0 us
  local copies, waits for them, and re-layouts: 7.9 us -> 3.4 us
  matrix products: 4.35 us -> 0 us
    pallas_call x2 -> x1, Pallas kernels: 148 us -> 159 us  [train(): pl.pallas_call(functools.partial(train_kernel, scale), in_specs=[smem, sm...]
    ppermute x4 -> x0, starting transfers between devices: 10.2 us -> none  [the longest x2 5.85 us: with_halo(): lax.ppermute(lax.slice_in_dim(block, block.shape[dim] - width, None, axis...]
    pallas_call x1, Pallas kernels: 5.78 us -> 12.9 us  [add_up(): pl.pallas_call(add_kernel, grid_spec=pltpu.PrefetchScalarGridSpec(num_sca...]
    ppermute x4 -> x0, waiting for transfers between devices: 4.96 us -> none  [the longest x2 4.95 us: with_halo(): lax.ppermute(lax.slice_in_dim(block, 0, width, axis=dim), axis, backward)]
    dot_general x3 -> x0, matrix products: 4.35 us -> none  [the longest x1 2.21 us: body(): lax.dot_general(patch_rows, dout, (((0,), (0,)), ((), ())), preferred_ele...]
    unnamed x21 -> x7, local copies, waits for them, and re-layouts: 6.92 us -> 2.61 us
  transfers between devices with their start and end apart: 4 -> 0, of which waited for: 2 -> 0; matrix products, arithmetic and copies ran while one was open for 1% -> 0% of each run, Pallas kernels for 0% -> 0%
where the time goes in v3:
time: 300 us
  Pallas kernels  174 us (58%)
  blocking collectives  119 us (40%)
  local copies, waits for them, and re-layouts  3.4 us (1%)
    pallas_call x1, Pallas kernels, train(): pl.pallas_call(functools.partial(train_kernel, scale), in_specs=[smem, sm...  159 us
    all_to_all x1, blocking collectives, body(): lax.all_to_all(outgoing, ('view', 'tile'), split_axis=0, concat_axis=0, t...  101 us
    all_to_all x1, blocking collectives, body(): lax.all_to_all(request, ('view', 'tile'), split_axis=0, concat_axis=0, ti...  17.4 us
    pallas_call x1, Pallas kernels, add_up(): pl.pallas_call(add_kernel, grid_spec=pltpu.PrefetchScalarGridSpec(num_sca...  12.9 us

profile of v3, /device:TPU:19, one launch (start us, length us, event | category | flops | bytes accessed | tf_op | source)
XLA Modules:
  0.0 299.6 jit_solution(11940032831885524075)
XLA Ops:
  0.6 0.7 fusion.1
  1.3 0.2 convert_reduce_fusion
  1.5 0.0 copy-start.2
  1.5 0.7 select_reduce_fusion
  2.2 0.1 sub.22
  2.3 17.4 %all_to_all.11 = s32[128,1,2]{2,1,0:T(1,128)S(1)} all-to-all(s32[128,1,2]{2,1,0:T(1,128)S(1)} %bitcast.23), channel_id=1, replica_groups=mesh['view'=4,'tile'=32] {'view','tile'}, dimensions={0} | all-to-all | bytes 2048 | tf_op jit(solution)/shard_map/all_to_all | solution.py:399
  19.7 0.5 broadcast.137
  20.2 0.8 reduce.3
  21.0 0.1 reshape.123
  21.2 0.6 broadcast_maximum_fusion
  21.8 0.0 copy-start
  21.8 1.6 copy-done
  23.4 1.3 shard_map.68
  24.7 0.0 copy-done.2
  24.7 101.5 %all_to_all.12 = bf16[128,2,128,128]{3,2,1,0:T(8,128)(2,1)} all-to-all(bf16[128,2,128,128]{3,2,1,0:T(8,128)(2,1)S(1)} %bitcast.18), channel_id=1, replica_groups=mesh['view'=4,'tile'=32] {'view','tile'}, dimensions={0} | all-to-all | bytes 16777216 | tf_op jit(solution)/shard_map/all_to_all | solution.py:402
  126.2 159.5 %shard_map.69 = (bf16[128,2,128,128]{3,2,1,0:T(8,128)(2,1)}, bf16[1152,512]{1,0:T(8,128)(2,1)}) custom-call(s32[128]{0:T(128)} %copy-done.2, s32[256]{0:T(256)} %get-tuple-element.6.listed_ref, bf16[512,16384]{1,0:T(8,128)(2,1)} %bitcast.20, bf16[256,128,128]{2,1,0:T(8,128)(2,1)} %bitcast.19, bf16[1152,512]{1,0:T(8,128)(2,1)} %dec_w_ref.1, ...), custom_call_target="tpu_custom_call" | custom-call | tf_op jit(solution)/shard_map/pallas_call | solution.py:310
  285.7 0.0 copy-start.1
  285.7 12.9 %shard_map.70 = f32[64,128,128]{2,1,0:T(8,128)} custom-call(s32[256]{0:T(256)} %get-tuple-element.11.idx_ref, bf16[256,128,128]{2,1,0:T(8,128)(2,1)} %bitcast.21), custom_call_target="tpu_custom_call" | custom-call | tf_op jit(solution)/shard_map/pallas_call | solution.py:364
  298.5 0.0 copy-done.1
  298.5 1.0 copy.10
  (2 shorter events, 0.0 us)
Async XLA Ops:
  1.5 23.2 %copy-start.2 = (s32[128]{0:T(128)}, s32[128]{0:T(128)S(1)}, u32[]{:S(2)}) copy-start(s32[128]{0:T(128)S(1)} %multiply_add_fusion.slot_ref) | copy-start | bytes 1540
  21.8 1.6 copy-start
  285.7 12.9 %copy-start.1 = (bf16[1152,512]{1,0:T(8,128)(2,1)S(1)}, bf16[1152,512]{1,0:T(8,128)(2,1)}, u32[]{:S(2)}) copy-start(bf16[1152,512]{1,0:T(8,128)(2,1)} %get-tuple-element.15) | copy-start | bytes 3538948

commit v4 on v3

--- a/solution.py
+++ b/solution.py
@@ -170,29 +170,29 @@
     image_grad = (later + spread[:, block : 2 * block] + earlier).astype(jnp.bfloat16)
     flipped = image_grad.astype(jnp.float32).T.astype(jnp.bfloat16)
 
-    def blocks_for(lin):
-        both = jnp.concatenate(
-            [w_ref[:, pl.ds(listed_ref[2 * lin + r] * block, block)] for r in range(2)], axis=1
-        )
-        made = jnp.dot(flipped, both, preferred_element_type=jnp.float32)
-        return [made[:, r * block : (r + 1) * block].T.astype(jnp.bfloat16) for r in range(2)]
-
-    def copy(step):
+    def block_for(lin, r):
+        some = w_ref[:, pl.ds(listed_ref[2 * lin + r] * block, block)]
+        return jnp.dot(flipped, some, preferred_element_type=jnp.float32).T.astype(jnp.bfloat16)
+
+    def copy(turn):
+        step = turn % (owners - 1) + 1
+        r = turn // (owners - 1)
         v, t = at_offset(step, n_view, n_tile)
         lin = v * n_tile + t
-        return lin, remote(
-            out_buf.at[lin], recv_ref.at[me], send_sem.at[step], recv_sem.at[step], v, t
-        )
-
-    def give(step, carry):
-        lin, sending = copy(step)
-        for r, made in enumerate(blocks_for(lin)):
-            out_buf[lin, r] = made
+        return lin, r, remote(
+            out_buf.at[lin, r], recv_ref.at[me, r], send_sem.at[turn], recv_sem.at[turn], v, t
+        )
+
+    def give(turn, carry):
+        lin, r, sending = copy(turn)
+        out_buf[lin, r] = block_for(lin, r)
         sending.start()
         return carry
 
-    lead = 8
-    lax.fori_loop(1, lead, give, 0)
+    turns = 2 * (owners - 1)
+
+    lead = 16
+    lax.fori_loop(0, lead, give, 0)
     for i in range(wide // 2):
         to_pair(i).wait()
 
@@ -219,7 +219,7 @@
     lax.fori_loop(1, chips, plane_out, 0)
     piece_buf[chip] = chip_sum(chip).astype(jnp.bfloat16)
 
-    middle = owners // 4
+    middle = owners // 2
     lax.fori_loop(lead, middle, give, 0)
 
     def plane_in(step, carry):
@@ -242,7 +242,7 @@
 
     for step in range(1, n_view):
         to_view(step).start()
-    second = owners // 2
+    second = owners
     lax.fori_loop(middle, second, give, 0)
     for step in range(1, n_view):
         to_view(step).wait()
@@ -266,9 +266,9 @@
         return carry
 
     lax.fori_loop(1, chips, spread_start, 0)
-    lax.fori_loop(second, owners, give, 0)
-    for r, made in enumerate(blocks_for(me)):
-        out_buf[me, r] = made
+    lax.fori_loop(second, turns, give, 0)
+    for r in range(2):
+        out_buf[me, r] = block_for(me, r)
     own_copy = pltpu.make_async_copy(out_buf.at[me], recv_ref.at[me], own_sem)
     own_copy.start()
 
@@ -287,10 +287,10 @@
         to_pair_end(i).start()
 
     def finish(step, carry):
-        copy(step)[1].wait()
-        return carry
-
-    lax.fori_loop(1, owners, finish, 0)
+        copy(step)[2].wait()
+        return carry
+
+    lax.fori_loop(0, turns, finish, 0)
     own_copy.wait()
     for i in range(wide // 2):
         to_pair_end(i).wait()
@@ -326,8 +326,8 @@
             pltpu.VMEM((n_tile // 2, high, chans), jnp.bfloat16),
             pltpu.VMEM((n_tile // 2, high, chans), jnp.bfloat16),
             pltpu.VMEM((n_view, high, chans), jnp.float32),
-            pltpu.SemaphoreType.DMA((owners,)),
-            pltpu.SemaphoreType.DMA((owners,)),
+            pltpu.SemaphoreType.DMA((2 * owners,)),
+            pltpu.SemaphoreType.DMA((2 * owners,)),
             pltpu.SemaphoreType.DMA((copies,)),
             pltpu.SemaphoreType.DMA((copies,)),
             pltpu.SemaphoreType.DMA((4,)),
@@ -338,44 +338,74 @@
     )(slot, listed, tile_w, arrived, decoder, target)
 
 
-def add_kernel(idx_ref, in_ref, out_ref, acc, sem):
-    step = pl.program_id(0)
+def add_kernel(idx_ref, in_ref, dec_in_ref, out_ref, dec_out_ref, buf, acc, dec_buf, in_sem, out_sem, dec_sem):
     count = in_ref.shape[0]
     owned = out_ref.shape[0]
-
-    @pl.when(step == 0)
-    def _():
-        acc[...] = jnp.zeros_like(acc)
-
-    for j in range(count):
-        where = idx_ref[step * count + j]
-        acc[where] += in_ref[j].astype(jnp.float32)
-
-    @pl.when(step == pl.num_programs(0) - 1)
-    def _():
-        copy = pltpu.make_async_copy(acc.at[pl.ds(0, owned)], out_ref, sem)
-        copy.start()
-        copy.wait()
-
-
-def add_up(index, received, owned):
+    loads, stores = in_sem.shape[0], out_sem.shape[0]
+    per, back = count // loads, owned // stores
+
+    def load(i):
+        return pltpu.make_async_copy(
+            in_ref.at[pl.ds(i * per, per)], buf.at[pl.ds(i * per, per)], in_sem.at[i]
+        )
+
+    def store(i):
+        return pltpu.make_async_copy(
+            acc.at[pl.ds(i * back, back)], out_ref.at[pl.ds(i * back, back)], out_sem.at[i]
+        )
+
+    for i in range(loads):
+        load(i).start()
+    dec_in = pltpu.make_async_copy(dec_in_ref, dec_buf, dec_sem.at[0])
+    dec_in.start()
+    acc[...] = jnp.zeros_like(acc)
+
+    for i in range(loads):
+        load(i).wait()
+
+        def one(j, carry):
+            where = idx_ref[j]
+
+            @pl.when(where >= 0)
+            def _():
+                acc[where] += buf[j].astype(jnp.float32)
+
+            return carry
+
+        lax.fori_loop(i * per, (i + 1) * per, one, 0, unroll=8)
+
+    for i in range(stores):
+        store(i).start()
+    dec_in.wait()
+    dec_out = pltpu.make_async_copy(dec_buf, dec_out_ref, dec_sem.at[1])
+    dec_out.start()
+    for i in range(stores):
+        store(i).wait()
+    dec_out.wait()
+
+
+def add_up(index, received, decoder_grad, owned):
     count, block, chans = received.shape
-    per = 16
+    loads, stores = 16, 8
+    hbm = pl.BlockSpec(memory_space=pl.ANY)
     return pl.pallas_call(
         add_kernel,
-        grid_spec=pltpu.PrefetchScalarGridSpec(
-            num_scalar_prefetch=1,
-            grid=(count // per,),
-            in_specs=[pl.BlockSpec((per, block, chans), lambda i, idx: (i, 0, 0))],
-            out_specs=pl.BlockSpec(memory_space=pl.ANY),
-            scratch_shapes=[
-                pltpu.VMEM((owned + 1, block, chans), jnp.float32),
-                pltpu.SemaphoreType.DMA,
-            ],
-        ),
-        out_shape=jax.ShapeDtypeStruct((owned, block, chans), jnp.float32),
-        compiler_params=pltpu.CompilerParams(vmem_limit_bytes=58 << 20),
-    )(index, received)
+        in_specs=[pl.BlockSpec(memory_space=pltpu.SMEM), hbm, hbm],
+        out_specs=[hbm, hbm],
+        scratch_shapes=[
+            pltpu.VMEM((count, block, chans), received.dtype),
+            pltpu.VMEM((owned, block, chans), jnp.float32),
+            pltpu.VMEM(decoder_grad.shape, decoder_grad.dtype),
+            pltpu.SemaphoreType.DMA((loads,)),
+            pltpu.SemaphoreType.DMA((stores,)),
+            pltpu.SemaphoreType.DMA((2,)),
+        ],
+        out_shape=[
+            jax.ShapeDtypeStruct((owned, block, chans), jnp.float32),
+            jax.ShapeDtypeStruct(decoder_grad.shape, decoder_grad.dtype),
+        ],
+        compiler_params=pltpu.CompilerParams(vmem_limit_bytes=56 << 20),
+    )(index, received, decoder_grad)
 
 
 def body(features, block_ids, weights, decoder, target):
@@ -408,8 +438,7 @@
         slot, in_slot, tile_w, arrived, decoder, target.reshape(pixels, -1), scale
     )
     received = received.reshape(owners * cap, block, chans)
-    feature_grad = add_up(jnp.where(incoming < 0, g_dev, incoming), received, g_dev)
-    return (feature_grad, decoder_grad)
+    return tuple(add_up(incoming, received, decoder_grad, g_dev))
 
 
 def solution(mesh):

time: 300 us -> 285 us (0.950); the launches traced: 300 us -> 281 us
  Pallas kernels: 174 us -> 157 us
    pallas_call x1, Pallas kernels: 159 us -> 148 us  [train(): pl.pallas_call(functools.partial(train_kernel, scale), in_specs=[smem, sm...]
    pallas_call x1, Pallas kernels: 12.9 us -> 7.25 us  [add_up(): pl.pallas_call(add_kernel, in_specs=[pl.BlockSpec(memory_space=pltpu.SMEM...]
where the time goes in v4:
time: 285 us; the launch traced here: 281 us
  Pallas kernels  157 us (55%)
  blocking collectives  119 us (42%)
    pallas_call x1, Pallas kernels, train(): pl.pallas_call(functools.partial(train_kernel, scale), in_specs=[smem, sm...  148 us
    all_to_all x1, blocking collectives, body(): lax.all_to_all(outgoing, ('view', 'tile'), split_axis=0, concat_axis=0, t...  101 us
    all_to_all x1, blocking collectives, body(): lax.all_to_all(request, ('view', 'tile'), split_axis=0, concat_axis=0, ti...  17.4 us
    pallas_call x1, Pallas kernels, add_up(): pl.pallas_call(add_kernel, in_specs=[pl.BlockSpec(memory_space=pltpu.SMEM...  7.25 us

profile of v4, /device:TPU:19, one launch (start us, length us, event | category | flops | bytes accessed | tf_op | source)
XLA Modules:
  0.0 281.0 jit_solution(11993206285998845152)
XLA Ops:
  0.6 0.7 fusion.1
  1.3 0.2 convert_reduce_fusion
  1.5 0.0 copy-start.2
  1.5 0.7 select_reduce_fusion
  2.2 0.1 sub.22
  2.3 17.4 %all_to_all.11 = s32[128,1,2]{2,1,0:T(1,128)S(1)} all-to-all(s32[128,1,2]{2,1,0:T(1,128)S(1)} %bitcast.23), channel_id=1, replica_groups=mesh['view'=4,'tile'=32] {'view','tile'}, dimensions={0} | all-to-all | bytes 2048 | tf_op jit(solution)/shard_map/all_to_all | solution.py:429
  19.7 0.5 broadcast.131
  20.2 0.8 reduce.3
  21.0 0.1 reshape.123.idx_ref
  21.2 0.0 copy-start.1
  21.2 0.0 copy-start
  21.2 1.6 copy-done
  22.8 1.3 shard_map.68
  24.1 0.0 copy-done.2
  24.1 0.0 copy-done.1
  24.1 101.5 %all_to_all.12 = bf16[128,2,128,128]{3,2,1,0:T(8,128)(2,1)} all-to-all(bf16[128,2,128,128]{3,2,1,0:T(8,128)(2,1)S(1)} %bitcast.18), channel_id=1, replica_groups=mesh['view'=4,'tile'=32] {'view','tile'}, dimensions={0} | all-to-all | bytes 16777216 | tf_op jit(solution)/shard_map/all_to_all | solution.py:432
  125.6 148.1 %shard_map.69 = (bf16[128,2,128,128]{3,2,1,0:T(8,128)(2,1)}, bf16[1152,512]{1,0:T(8,128)(2,1)}) custom-call(s32[128]{0:T(128)} %copy-done.2, s32[256]{0:T(256)} %get-tuple-element.6.listed_ref, bf16[512,16384]{1,0:T(8,128)(2,1)} %bitcast.20, bf16[256,128,128]{2,1,0:T(8,128)(2,1)} %bitcast.19, bf16[1152,512]{1,0:T(8,128)(2,1)} %dec_w_ref.1, ...), custom_call_target="tpu_custom_call" | custom-call | tf_op jit(solution)/shard_map/pallas_call | solution.py:310
  273.7 7.2 %shard_map.70 = (f32[64,128,128]{2,1,0:T(8,128)}, bf16[1152,512]{1,0:T(8,128)(2,1)}) custom-call(s32[256]{0:T(256)} %copy-done.1, bf16[256,128,128]{2,1,0:T(8,128)(2,1)} %bitcast.21, bf16[1152,512]{1,0:T(8,128)(2,1)} %get-tuple-element.5.dec_in_ref), custom_call_target="tpu_custom_call" | custom-call | tf_op jit(solution)/shard_map/pallas_call | solution.py:391
  (3 shorter events, 0.0 us)
Async XLA Ops:
  1.5 22.6 %copy-start.2 = (s32[128]{0:T(128)}, s32[128]{0:T(128)S(1)}, u32[]{:S(2)}) copy-start(s32[128]{0:T(128)S(1)} %multiply_add_fusion.slot_ref) | copy-start | bytes 1540
  21.2 3.0 %copy-start.1 = (s32[256]{0:T(256)}, s32[256]{0:T(256)S(1)}, u32[]{:S(2)}) copy-start(s32[256]{0:T(256)S(1)} %reshape.123.idx_ref) | copy-start | bytes 3076
  21.2 1.6 copy-start

commit v5 on v4

--- a/solution.py
+++ b/solution.py
@@ -48,10 +48,11 @@
 
 
 def train_kernel(
-    scale, slot_ref, listed_ref, w_ref, arrived_ref, dec_w_ref, target_ref, recv_ref, dec_ref,
-    acc, rows_buf, target_buf, part_ref,
+    scale, slot_ref, listed_ref, w_hbm, arrived_hbm, dec_w_hbm, target_hbm, recv_ref, dec_ref,
+    w_ref, arrived_ref, dec_w_ref, acc, rows_buf, target_buf, part_ref,
     out_buf, pair_buf, mine_buf, piece_buf, send_buf, view_buf,
     send_sem, recv_sem, dec_send, dec_recv, halo_send, halo_recv, own_sem,
+    block_sem, weight_sem, other_sem,
 ):
     n_view, n_tile = lax.axis_size("view"), lax.axis_size("tile")
     owners = n_view * n_tile
@@ -77,6 +78,41 @@
     def rows(j):
         return pl.ds(pl.multiple_of(j * high, 16), high)
 
+    group = GROUP * block
+    groups = w_ref.shape[1] // group
+    few = arrived_ref.shape[0] // block_sem.shape[0]
+
+    def block_load(i):
+        part = pl.ds(i * few, few)
+        return pltpu.make_async_copy(arrived_hbm.at[part], arrived_ref.at[part], block_sem.at[i])
+
+    def weight_load(i):
+        part = pl.ds(pl.multiple_of(i * group, group), group)
+        return pltpu.make_async_copy(w_hbm.at[:, part], w_ref.at[:, part], weight_sem.at[i])
+
+    others = [
+        pltpu.make_async_copy(dec_w_hbm, dec_w_ref, other_sem.at[0]),
+        pltpu.make_async_copy(target_hbm, target_buf.at[pl.ds(width, pixels)], other_sem.at[1]),
+    ]
+    for i in range(block_sem.shape[0]):
+        block_load(i).start()
+    for i in range(groups):
+        weight_load(i).start()
+    for one in others:
+        one.start()
+
+    barrier = pltpu.get_barrier_semaphore()
+
+    def greet(step, carry):
+        v = lax.rem(view + lax.div(step, n_tile), n_view)
+        t = lax.rem(tile + lax.rem(step, n_tile), n_tile)
+        pl.semaphore_signal(
+            barrier, inc=1, device_id=(v, t), device_id_type=pl.DeviceIdType.MESH
+        )
+        return carry
+
+    lax.fori_loop(1, owners, greet, 0)
+
     right, left = (tile + 1) % n_tile, (tile + n_tile - 1) % n_tile
     two = 2 * width
 
@@ -86,33 +122,35 @@
             halo_send.at[i], halo_recv.at[i], view, to,
         )
 
-    target_buf[width : width + pixels, :] = target_ref[...]
     target_halos = [
         halo(target_buf, 0, pixels, width, 0, right),
         halo(target_buf, 1, width, width, width + pixels, left),
     ]
-    for one in target_halos:
-        one.start()
-
     acc[...] = jnp.zeros_like(acc)
+    for i in range(block_sem.shape[0]):
+        block_load(i).wait()
 
     def add_group(i, carry):
+        weight_load(i).wait()
         stacked = jnp.concatenate(
             [arrived_ref[slot_ref[i * GROUP + j]] for j in range(GROUP)], axis=0
         )
-        columns = pl.ds(pl.multiple_of(i * (GROUP * block), GROUP * block), GROUP * block)
+        columns = pl.ds(pl.multiple_of(i * group, group), group)
         acc[...] += jnp.dot(w_ref[:, columns], stacked, preferred_element_type=jnp.float32)
         return carry
 
-    lax.fori_loop(0, w_ref.shape[1] // (GROUP * block), add_group, 0)
+    lax.fori_loop(0, groups, add_group, 0)
+    for one in others:
+        one.wait()
     rows_buf[two : two + pixels, :] = acc[...].astype(jnp.bfloat16)
     image_halos = [
         halo(rows_buf, 2, pixels, two, 0, right),
         halo(rows_buf, 3, two, two, two + pixels, left),
     ]
-    for one in image_halos:
+    pl.semaphore_wait(barrier, owners - 1)
+    for one in image_halos + target_halos:
         one.start()
-    for one in target_halos + image_halos:
+    for one in image_halos + target_halos:
         one.wait()
 
     padded = pixels + 4 * width
@@ -307,15 +345,20 @@
     copies = wide // 2 + n_tile // 2 + n_view + n_tile // 2 + wide // 2
     vmem = pl.BlockSpec(memory_space=pltpu.VMEM)
     smem = pl.BlockSpec(memory_space=pltpu.SMEM)
+    hbm = pl.BlockSpec(memory_space=pl.ANY)
+    groups = tile_w.shape[1] // (GROUP * chans)
     return pl.pallas_call(
         functools.partial(train_kernel, scale),
-        in_specs=[smem, smem, vmem, vmem, vmem, vmem],
-        out_specs=[pl.BlockSpec(memory_space=pl.ANY), vmem],
+        in_specs=[smem, smem, hbm, hbm, hbm, hbm],
+        out_specs=[hbm, vmem],
         out_shape=[
             jax.ShapeDtypeStruct((owners, 2, chans, chans), jnp.bfloat16),
             jax.ShapeDtypeStruct((deep, outs), jnp.bfloat16),
         ],
         scratch_shapes=[
+            pltpu.VMEM(tile_w.shape, tile_w.dtype),
+            pltpu.VMEM(arrived.shape, arrived.dtype),
+            pltpu.VMEM(decoder.shape, decoder.dtype),
             pltpu.VMEM((pixels, chans), jnp.float32),
             pltpu.VMEM((pixels + 4 * chans, chans), jnp.bfloat16),
             pltpu.VMEM((pixels + 2 * chans, outs), jnp.bfloat16),
@@ -333,8 +376,13 @@
             pltpu.SemaphoreType.DMA((4,)),
             pltpu.SemaphoreType.DMA((4,)),
             pltpu.SemaphoreType.DMA,
+            pltpu.SemaphoreType.DMA((8,)),
+            pltpu.SemaphoreType.DMA((groups,)),
+            pltpu.SemaphoreType.DMA((2,)),
         ],
-        compiler_params=pltpu.CompilerParams(has_side_effects=True, vmem_limit_bytes=58 << 20),
+        compiler_params=pltpu.CompilerParams(
+            collective_id=0, has_side_effects=True, vmem_limit_bytes=58 << 20
+        ),
     )(slot, listed, tile_w, arrived, decoder, target)
 
 

time: 285 us -> 281 us (0.986)
  Pallas kernels: 157 us -> 153 us
    pallas_call x1, Pallas kernels: 148 us -> 144 us  [train(): pl.pallas_call(functools.partial(train_kernel, scale), in_specs=[smem, sm...]
where the time goes in v5:
time: 281 us; the launch traced here: 277 us
  Pallas kernels  153 us (54%)
  blocking collectives  119 us (42%)
    pallas_call x1, Pallas kernels, train(): pl.pallas_call(functools.partial(train_kernel, scale), in_specs=[smem, sm...  144 us
    all_to_all x1, blocking collectives, body(): lax.all_to_all(outgoing, ('view', 'tile'), split_axis=0, concat_axis=0, t...  101 us
    all_to_all x1, blocking collectives, body(): lax.all_to_all(request, ('view', 'tile'), split_axis=0, concat_axis=0, ti...  17.4 us
    pallas_call x1, Pallas kernels, add_up(): pl.pallas_call(add_kernel, in_specs=[pl.BlockSpec(memory_space=pltpu.SMEM...  7.27 us

profile of v5, /device:TPU:19, one launch (start us, length us, event | category | flops | bytes accessed | tf_op | source)
XLA Modules:
  0.0 277.0 jit_solution(12717851909417836638)
XLA Ops:
  0.6 0.7 fusion.1
  1.3 0.2 convert_reduce_fusion
  1.5 0.0 copy-start.2
  1.5 0.7 select_reduce_fusion
  2.2 0.1 sub.22
  2.3 17.4 %all_to_all.11 = s32[128,1,2]{2,1,0:T(1,128)S(1)} all-to-all(s32[128,1,2]{2,1,0:T(1,128)S(1)} %bitcast.23), channel_id=1, replica_groups=mesh['view'=4,'tile'=32] {'view','tile'}, dimensions={0} | all-to-all | bytes 2048 | tf_op jit(solution)/shard_map/all_to_all | solution.py:477
  19.7 0.5 broadcast.131
  20.2 0.8 reduce.3
  21.0 0.1 reshape.123.idx_ref
  21.2 0.0 copy-start.1
  21.2 0.0 copy-start
  21.2 1.6 copy-done
  22.8 1.3 shard_map.68
  24.1 0.0 copy-done.2
  24.1 0.0 copy-done.1
  24.1 101.5 %all_to_all.12 = bf16[128,2,128,128]{3,2,1,0:T(8,128)(2,1)} all-to-all(bf16[128,2,128,128]{3,2,1,0:T(8,128)(2,1)S(1)} %bitcast.18), channel_id=1, replica_groups=mesh['view'=4,'tile'=32] {'view','tile'}, dimensions={0} | all-to-all | bytes 16777216 | tf_op jit(solution)/shard_map/all_to_all | solution.py:480
  125.6 144.1 %shard_map.69 = (bf16[128,2,128,128]{3,2,1,0:T(8,128)(2,1)}, bf16[1152,512]{1,0:T(8,128)(2,1)}) custom-call(s32[128]{0:T(128)} %copy-done.2, s32[256]{0:T(256)} %get-tuple-element.6.listed_ref, bf16[512,16384]{1,0:T(8,128)(2,1)} %bitcast.20, bf16[256,128,128]{2,1,0:T(8,128)(2,1)} %bitcast.19, bf16[1152,512]{1,0:T(8,128)(2,1)} %dec_w_hbm.1, ...), custom_call_target="tpu_custom_call" | custom-call | tf_op jit(solution)/shard_map/pallas_call | solution.py:350
  269.7 7.3 %shard_map.70 = (f32[64,128,128]{2,1,0:T(8,128)}, bf16[1152,512]{1,0:T(8,128)(2,1)}) custom-call(s32[256]{0:T(256)} %copy-done.1, bf16[256,128,128]{2,1,0:T(8,128)(2,1)} %bitcast.21, bf16[1152,512]{1,0:T(8,128)(2,1)} %get-tuple-element.5.dec_in_ref), custom_call_target="tpu_custom_call" | custom-call | tf_op jit(solution)/shard_map/pallas_call | solution.py:439
  (3 shorter events, 0.0 us)
Async XLA Ops:
  1.5 22.6 %copy-start.2 = (s32[128]{0:T(128)}, s32[128]{0:T(128)S(1)}, u32[]{:S(2)}) copy-start(s32[128]{0:T(128)S(1)} %multiply_add_fusion.slot_ref) | copy-start | bytes 1540
  21.2 3.0 %copy-start.1 = (s32[256]{0:T(256)}, s32[256]{0:T(256)S(1)}, u32[]{:S(2)}) copy-start(s32[256]{0:T(256)S(1)} %reshape.123.idx_ref) | copy-start | bytes 3076
  21.2 1.6 copy-start

commit v6 on v5

--- a/solution.py
+++ b/solution.py
@@ -38,13 +38,15 @@
 def at_offset(step, n_view, n_tile):
     view, tile = lax.axis_index("view"), lax.axis_index("tile")
     side = n_view
-    rest = step % (n_view * n_tile // 2)
-    first, second, third = rest % side, (rest // side) % side, rest // (side * side)
-    core = (step // (n_view * n_tile // 2) + step) % 2
-    y, x, c = tile // (2 * side), (tile // 2) % side, tile % 2
-    to_y = (y + first + second) % side
-    to_x = (x + first + third + 2 * second) % side
-    return (view + first) % side, (to_y * side + to_x) * 2 + (c + core) % 2
+    rem, div = lax.rem, lax.div
+    half = n_view * n_tile // 2
+    rest = rem(step, half)
+    first, second, third = rem(rest, side), rem(div(rest, side), side), div(rest, side * side)
+    core = rem(div(step, half) + step, 2)
+    y, x, c = div(tile, 2 * side), rem(div(tile, 2), side), rem(tile, 2)
+    to_y = rem(y + first + second, side)
+    to_x = rem(x + first + third + 2 * second, side)
+    return rem(view + first, side), (to_y * side + to_x) * 2 + rem(c + core, 2)
 
 
 def train_kernel(
@@ -213,8 +215,8 @@
         return jnp.dot(flipped, some, preferred_element_type=jnp.float32).T.astype(jnp.bfloat16)
 
     def copy(turn):
-        step = turn % (owners - 1) + 1
-        r = turn // (owners - 1)
+        step = lax.rem(turn, owners - 1) + 1
+        r = lax.div(turn, owners - 1)
         v, t = at_offset(step, n_view, n_tile)
         lin = v * n_tile + t
         return lin, r, remote(

time: 281 us -> 281 us (level)
  no operation moved by 1% of the time
where the time goes in v6:
time: 281 us; the launch traced here: 276 us
  Pallas kernels  152 us (54%)
  blocking collectives  119 us (42%)
    pallas_call x1, Pallas kernels, train(): pl.pallas_call(functools.partial(train_kernel, scale), in_specs=[smem, sm...  143 us
    all_to_all x1, blocking collectives, body(): lax.all_to_all(outgoing, ('view', 'tile'), split_axis=0, concat_axis=0, t...  101 us
    all_to_all x1, blocking collectives, body(): lax.all_to_all(request, ('view', 'tile'), split_axis=0, concat_axis=0, ti...  17.4 us
    pallas_call x1, Pallas kernels, add_up(): pl.pallas_call(add_kernel, in_specs=[pl.BlockSpec(memory_space=pltpu.SMEM...  7.18 us

profile of v6, /device:TPU:19, one launch (start us, length us, event | category | flops | bytes accessed | tf_op | source)
XLA Modules:
  0.0 276.0 jit_solution(11564294107720269145)
XLA Ops:
  0.6 0.7 fusion.1
  1.3 0.2 convert_reduce_fusion
  1.5 0.0 copy-start.2
  1.5 0.7 select_reduce_fusion
  2.2 0.1 sub.22
  2.3 17.4 %all_to_all.11 = s32[128,1,2]{2,1,0:T(1,128)S(1)} all-to-all(s32[128,1,2]{2,1,0:T(1,128)S(1)} %bitcast.23), channel_id=1, replica_groups=mesh['view'=4,'tile'=32] {'view','tile'}, dimensions={0} | all-to-all | bytes 2048 | tf_op jit(solution)/shard_map/all_to_all | solution.py:479
  19.7 0.5 broadcast.131
  20.2 0.8 reduce.3
  21.0 0.1 reshape.123.idx_ref
  21.2 0.0 copy-start.1
  21.2 0.0 copy-start
  21.2 1.6 copy-done
  22.8 1.3 shard_map.68
  24.1 0.0 copy-done.2
  24.1 0.0 copy-done.1
  24.1 101.5 %all_to_all.12 = bf16[128,2,128,128]{3,2,1,0:T(8,128)(2,1)} all-to-all(bf16[128,2,128,128]{3,2,1,0:T(8,128)(2,1)S(1)} %bitcast.18), channel_id=1, replica_groups=mesh['view'=4,'tile'=32] {'view','tile'}, dimensions={0} | all-to-all | bytes 16777216 | tf_op jit(solution)/shard_map/all_to_all | solution.py:482
  125.6 143.2 %shard_map.69 = (bf16[128,2,128,128]{3,2,1,0:T(8,128)(2,1)}, bf16[1152,512]{1,0:T(8,128)(2,1)}) custom-call(s32[128]{0:T(128)} %copy-done.2, s32[256]{0:T(256)} %get-tuple-element.6.listed_ref, bf16[512,16384]{1,0:T(8,128)(2,1)} %bitcast.20, bf16[256,128,128]{2,1,0:T(8,128)(2,1)} %bitcast.19, bf16[1152,512]{1,0:T(8,128)(2,1)} %dec_w_hbm.1, ...), custom_call_target="tpu_custom_call" | custom-call | tf_op jit(solution)/shard_map/pallas_call | solution.py:352
  268.8 7.2 %shard_map.70 = (f32[64,128,128]{2,1,0:T(8,128)}, bf16[1152,512]{1,0:T(8,128)(2,1)}) custom-call(s32[256]{0:T(256)} %copy-done.1, bf16[256,128,128]{2,1,0:T(8,128)(2,1)} %bitcast.21, bf16[1152,512]{1,0:T(8,128)(2,1)} %get-tuple-element.5.dec_in_ref), custom_call_target="tpu_custom_call" | custom-call | tf_op jit(solution)/shard_map/pallas_call | solution.py:441
  (3 shorter events, 0.0 us)
Async XLA Ops:
  1.5 22.6 %copy-start.2 = (s32[128]{0:T(128)}, s32[128]{0:T(128)S(1)}, u32[]{:S(2)}) copy-start(s32[128]{0:T(128)S(1)} %multiply_add_fusion.slot_ref) | copy-start | bytes 1540
  21.2 3.0 %copy-start.1 = (s32[256]{0:T(256)}, s32[256]{0:T(256)S(1)}, u32[]{:S(2)}) copy-start(s32[256]{0:T(256)S(1)} %reshape.123.idx_ref) | copy-start | bytes 3076
  21.2 1.6 copy-start
